TPU v7x, 256 devices: a whole 4x4x8 slice. The times are simulated.
256 devices in a mesh: prow: 16 (over y, x), pcol: 16 (over z, core).
Axes of the slice: x: 4, y: 4, z: 8, core: 2. Of those that a mesh axis runs over, the one named last changes fastest.
Arguments:
- trailing: float32 [2, 8192, 2, 8192], P(None, 'prow', None, 'pcol'), may hold values from -6 to 6
- panel: float32 [2, 8192, 512], P(None, 'prow', 'pcol'), may hold values from -4 to 4
- diag_inverse: float32 [512, 512], replicated, as said below
Outputs:
- updated: float32 [2, 8192, 2, 8192], P(None, 'prow', None, 'pcol')
- factor: float32 [2, 8192, 512], P(None, 'prow', 'pcol')
Inputs may be any that keep to these rules, and one draw needn't show every extreme that they name: `diag_inverse`: the inverse of the lower Cholesky factor of the leading 512 x 512 block; zero above its diagonal.
All inputs are finite; a program needn't handle non-finite values.
Results may differ from a plain program's by a relative error of at most 0.0003.
Values sent between devices are 32-bit elements; how exact they have to be, the bound alone decides.
No kernel may reach another device: no remote copies, remote signals or barrier semaphores. Data moves between devices by JAX's collectives and lax.ppermute only.
A program may use at most 64 MiB of HBM per device.

v0:
```python
import jax
import jax.numpy as jnp
from jax import lax
from jax.sharding import PartitionSpec as P


def update_tile(current, left_tile, right_tile, beneath):

    def changed():
        return current - jnp.dot(
            left_tile,
            right_tile.T,
            precision=lax.Precision.HIGHEST,
            preferred_element_type=jnp.float32,
        )

    def skipped():
        return jnp.zeros_like(current)

    return lax.cond(beneath, changed, skipped)


def local(trailing, panel, diag_inverse):
    rounds, width, tcount, _ = trailing.shape
    narrow = panel.shape[2]
    prow_id = lax.axis_index("prow")
    pcol_id = lax.axis_index("pcol")
    row_groups = lax.axis_size("prow")
    col_groups = lax.axis_size("pcol")
    shard_part = lax.all_gather(panel, "pcol", axis=2, tiled=True)
    columns_here = shard_part.shape[2]
    flat_part = shard_part.reshape(rounds * width, columns_here)
    factor = jnp.dot(
        flat_part,
        diag_inverse.T,
        precision=lax.Precision.HIGHEST,
        preferred_element_type=jnp.float32,
    )
    own_columns = lax.dynamic_slice_in_dim(factor, pcol_id * narrow, narrow, 1).reshape(
        rounds, width, narrow
    )
    factor_tiles = factor.reshape(rounds, width, width)
    wanted = jnp.arange(tcount, dtype=jnp.int32) * col_groups + pcol_id
    local_round = jnp.minimum(wanted // row_groups, rounds - 1)
    present = wanted % row_groups == prow_id
    picked = jnp.take(factor_tiles, local_round, axis=0) * present[:, None, None].astype(
        jnp.float32
    )
    mirror = lax.psum(picked, "prow")
    row_tile = jnp.arange(rounds, dtype=jnp.int32) * row_groups + prow_id
    new_rows = []
    for round_a in range(rounds):
        row_pieces = []
        for round_b in range(tcount):
            beneath = row_tile[round_a] >= wanted[round_b]
            row_pieces.append(
                update_tile(
                    trailing[round_a, :, round_b, :],
                    factor_tiles[round_a],
                    mirror[round_b],
                    beneath,
                )
            )
        new_rows.append(jnp.stack(row_pieces, axis=1))
    result = jnp.stack(new_rows, axis=0)
    return (result, own_columns)


def solution(mesh):
    return jax.shard_map(
        local,
        mesh=mesh,
        in_specs=(P(None, "prow", None, "pcol"), P(None, "prow", "pcol"), P()),
        out_specs=(P(None, "prow", None, "pcol"), P(None, "prow", "pcol")),
        check_vma=False,
    )
```

profile of v0, /device:TPU:6, one launch (start us, length us, event | category | flops | bytes accessed | tf_op | source)
XLA Modules:
  0.0 206.9 jit_solution(15825225145605241511)
XLA Ops:
  7.2 0.0 copy-start
  7.2 0.0 all-gather.2.cloned.1.call-start
  7.2 1.7 copy.24
  9.0 0.0 all-gather.2.cloned.1.call-update
  9.0 0.0 all-reduce.2.cloned.1.call-start
  9.1 44.0 %all-gather.2.cloned.1.call-done = f32[2,512,512]{1,0,2:T(2,128)} async-done(((f32[2,512,32]{1,0,2:T(2,128)}), f32[2,512,512]{1,0,2:T(2,128)}) %all-gather.2.cloned.1.call-update) | async-done | bytes 2097168 | tf_op jit(solution)/shard_map/all_gather | solution.py:30
  53.1 4.1 %copy.25 = f32[2,512,512]{2,1,0:T(8,128)} copy(f32[2,512,512]{1,0,2:T(2,128)} %all-gather.2.cloned.1.call-done) | data formatting | bytes 4194304 | tf_op jit(solution)/shard_map/all_gather | solution.py:30
  57.2 0.0 copy-done
  57.2 5.0 %fusion.10 = f32[1024,512]{1,0:T(8,128)S(1)} fusion(f32[1024,512]{1,0:T(8,128)} %bitcast.52, f32[512,512]{1,0:T(8,128)S(1)} %copy-done), kind=kOutput, calls=%fused_computation.41 | convolution fusion | flops 3221225472 | bytes 5242880 | tf_op jit(solution)/shard_map/dot_general | solution.py:33
  62.3 2.0 gather_fusion
  64.3 3.2 %select_multiply_fusion = f32[2,512,512]{2,1,0:T(8,128)} fusion(f32[2,512,512]{2,1,0:T(8,128)} %gather_fusion, f32[2]{0:T(128)S(1)} %get-tuple-element.114, pred[2]{0:T(512)(128)(4,1)S(1)} %get-tuple-element.115), kind=kLoop, calls=%fused_computation.16 | loop fusion | flops 1048576 | bytes 4194314 | tf_op jit(solution)/shard_map/mul | solution.py:46
  67.5 0.0 all-reduce.2.cloned.1.call-update
  67.5 0.7 fusion.8
  73.4 1.0 constant_dynamic-slice_fusion
  74.4 1.9 copy.35
  76.3 1.6 fusion.7
  77.9 88.2 %all-reduce.2.cloned.1.call-done = f32[2,512,512]{2,1,0:T(8,128)} async-done(((f32[2,512,512]{2,1,0:T(8,128)}), f32[2,512,512]{2,1,0:T(8,128)}) %all-reduce.2.cloned.1.call-update) | async-done | bytes 2097168 | tf_op jit(solution)/shard_map/psum | solution.py:49
  166.1 2.9 %slice_bitcast_fusion.5 = (f32[512,512]{1,0:T(8,128)}, f32[512,512]{1,0:T(8,128)S(1)}) fusion(f32[2,512,512]{2,1,0:T(8,128)} %all-reduce.2.cloned.1.call-done), kind=kLoop, calls=%fused_computation.18 | loop fusion | bytes 4194304 | tf_op jit(solution)/shard_map/squeeze | solution.py:60
  168.9 0.0 copy-done.1
  168.9 5.4 %conditional.6 = (f32[512,1,512]{2,1,0:T(1,128)S(1)}) conditional(s32[]{:T(128)} %bitcast.16, () %tuple.44, (f32[2,512,2,512]{3,2,1,0:T(2,128)S(1)}, f32[512,512]{1,0:T(8,128)}, f32[512,512]{1,0:T(8,128)}) %tuple.90), branch_computations={%region_5.6_spmd, %region_6.7_spmd} | conditional | flops 1610874880 | bytes 18874404 | solution.py:20
  168.9 0.8 copy.30
  169.8 0.4 copy-done.4
  170.2 3.1 %fusion.2 = f32[512,1,512]{2,0,1:T(8,128)S(1)} fusion(f32[512,512]{1,0:T(8,128)S(1)} %copy-done.4, f32[512,512]{1,0:T(8,128)} %get-tuple-element.56, f32[2,512,2,512]{3,1,2,0:T(8,128)S(1)} %copy.30), kind=kOutput, calls=%fused_computation.8 | convolution fusion | flops 1610874880 | bytes 4194304 | tf_op jit(solution)/shard_map/cond/branch_1_fun/dot_general | solution.py:10
  173.3 1.1 copy.43
  174.4 0.0 copy-start.7
  174.4 0.0 copy-start.3
  174.4 1.0 copy-done.7
  175.4 6.1 %conditional.7 = (f32[512,1,512]{2,1,0:T(1,128)S(1)}) conditional(s32[]{:T(128)} %bitcast.17, () %tuple.46, (f32[2,512,2,512]{3,2,1,0:T(2,128)}, f32[512,512]{1,0:T(8,128)}, f32[512,512]{1,0:T(8,128)S(1)}) %tuple.47), branch_computations={%region_7.8_spmd, %region_8.9_spmd} | conditional | flops 1610874880 | bytes 18874404 | solution.py:20
  175.4 3.1 %copy.31 = f32[2,512,2,512]{3,1,2,0:T(8,128)S(1)} copy(f32[2,512,2,512]{3,2,1,0:T(2,128)} %get-tuple-element.97) | data formatting | bytes 8388608 | tf_op jit(solution)/shard_map
  178.5 0.0 copy-done.5
  178.5 1.9 fusion.3
  180.3 1.1 copy.45
  181.4 0.0 copy-start.2
  181.4 4.6 %maximum_bitcast_fusion.1 = f32[1,512,2,512]{3,2,1,0:T(2,128)} fusion(f32[512,1,512]{2,1,0:T(1,128)S(1)} %get-tuple-element.105, f32[512,1,512]{2,1,0:T(1,128)} %copy-done.7), kind=kLoop, calls=%fused_computation.15 | loop fusion | flops 524288 | bytes 4194304 | tf_op jit(solution)/shard_map/stack | solution.py:65
  186.0 0.0 copy-done.3
  186.0 0.0 copy-done.2
  186.0 5.0 %conditional.4 = (f32[512,1,512]{2,1,0:T(1,128)S(1)}) conditional(s32[]{:T(128)} %bitcast.8, () %tuple.40, (f32[2,512,2,512]{3,2,1,0:T(2,128)S(1)}, f32[512,512]{1,0:T(8,128)S(1)}, f32[512,512]{1,0:T(8,128)}) %tuple.92), branch_computations={%region_1.2_spmd, %region_2.3_spmd} | conditional | flops 1610874880 | bytes 14680072 | solution.py:20
  186.0 0.8 copy.26
  186.8 3.1 %fusion = f32[512,1,512]{2,0,1:T(8,128)S(1)} fusion(f32[512,512]{1,0:T(8,128)S(1)} %get-tuple-element.49, f32[512,512]{1,0:T(8,128)} %get-tuple-element.50, f32[2,512,2,512]{3,1,2,0:T(8,128)S(1)} %copy.26), kind=kOutput, calls=%fused_computation.2 | convolution fusion | flops 1610874880 | bytes 4194304 | tf_op jit(solution)/shard_map/cond/branch_1_fun/dot_general | solution.py:10
  190.0 1.1 copy.39
  191.0 0.0 copy-start.8
  191.1 1.0 copy-done.8
  192.0 0.8 conditional.5
  192.0 0.5 stack.32.clone
  192.8 0.0 copy-start.6
  192.8 3.3 %maximum_bitcast_fusion = f32[1,512,2,512]{3,2,1,0:T(2,128)S(1)} fusion(f32[512,1,512]{2,1,0:T(1,128)S(1)} %get-tuple-element.103, f32[512,1,512]{2,1,0:T(1,128)} %copy-done.8), kind=kLoop, calls=%fused_computation.14 | loop fusion | flops 524288 | bytes 4194304 | tf_op jit(solution)/shard_map/stack | solution.py:65
  196.1 0.0 copy-done.6
  196.1 4.0 %pad_maximum_fusion = f32[2,512,2,512]{3,2,1,0:T(2,128)} fusion(f32[1,512,2,512]{3,2,1,0:T(2,128)S(1)} %copy-done.6, f32[1,512,2,512]{3,2,1,0:T(2,128)S(1)} %maximum_bitcast_fusion), kind=kLoop, calls=%fused_computation.13 | loop fusion | flops 1048576 | bytes 8388608 | tf_op jit(solution)/shard_map/stack | solution.py:65
  (8 shorter events, 0.1 us)
Async XLA Ops:
  7.2 50.0 %copy-start = (f32[512,512]{1,0:T(8,128)S(1)}, f32[512,512]{1,0:T(8,128)}, u32[]{:S(2)}) copy-start(f32[512,512]{1,0:T(8,128)} %param.13) | copy-start | bytes 3145732
  7.2 45.9 %all-gather.2.cloned.1.call-start = ((), (), s32[]{:S(2)}) async-start(), calls=%async_computation | async-start | bytes 2228224 | tf_op jit(solution)/shard_map/all_gather | solution.py:30
  9.0 157.1 %all-reduce.2.cloned.1.call-start = ((), (), s32[]{:S(2)}) async-start(), calls=%async_computation.1 | async-start | bytes 4194304 | tf_op jit(solution)/shard_map/psum | solution.py:49
  166.1 2.9 %copy-start.1 = (f32[2,512,2,512]{3,2,1,0:T(2,128)S(1)}, f32[2,512,2,512]{3,2,1,0:T(2,128)}, u32[]{:S(2)}) copy-start(f32[2,512,2,512]{3,2,1,0:T(2,128)} %param.11) | copy-start | bytes 12582916
  168.9 1.2 copy-start.4
  174.4 1.0 copy-start.7
  174.4 11.6 %copy-start.3 = (f32[512,512]{1,0:T(8,128)S(1)}, f32[512,512]{1,0:T(8,128)}, u32[]{:S(2)}) copy-start(f32[512,512]{1,0:T(8,128)} %get-tuple-element.106) | copy-start | bytes 3145732
  175.4 3.1 %copy-start.5 = (f32[512,512]{1,0:T(8,128)S(1)}, f32[512,512]{1,0:T(8,128)}, u32[]{:S(2)}) copy-start(f32[512,512]{1,0:T(8,128)} %get-tuple-element.58) | copy-start | bytes 3145732 | tf_op jit(solution)/shard_map/cond
  181.4 4.6 %copy-start.2 = (f32[2,512,2,512]{3,2,1,0:T(2,128)S(1)}, f32[2,512,2,512]{3,2,1,0:T(2,128)}, u32[]{:S(2)}) copy-start(f32[2,512,2,512]{3,2,1,0:T(2,128)} %param.11) | copy-start | bytes 12582916
  191.0 1.0 copy-start.8
  192.8 3.3 %copy-start.6 = (f32[1,512,2,512]{3,2,1,0:T(2,128)S(1)}, f32[1,512,2,512]{3,2,1,0:T(2,128)}, u32[]{:S(2)}) copy-start(f32[1,512,2,512]{3,2,1,0:T(2,128)} %maximum_bitcast_fusion.1) | copy-start | bytes 6291460
Sparse Core Ops, SparseCore 0:
  10.4 42.6 all-gather.1
  67.6 98.3 all-reduce.1
where the time goes:
time: 207 us
  waiting for transfers between devices  132 us (64%)
  local copies, waits for them, and re-layouts  26.7 us (13%)
  between operations  19.4 us (9%)
  other arithmetic  15.1 us (7%)
  matrix products  13.1 us (6%)
    psum x1, waiting for transfers between devices, local(): mirror = lax.psum(picked, 'prow')  88.2 us
    all_gather x1, waiting for transfers between devices, local(): shard_part = lax.all_gather(panel, 'pcol', axis=2, tiled=True)  44 us
    another operation x3, other arithmetic, local(): result = jnp.stack(new_rows, axis=0)  11.8 us
    dot_general x3, matrix products, changed(): jnp.dot(left_tile, right_tile.T, precision=lax.Precision.HIGHEST, preferr...  8.08 us
    unnamed x16, local copies, waits for them, and re-layouts  5.6 us
    dot_general x1, matrix products, local(): jnp.dot(flat_part, diag_inverse.T, precision=lax.Precision.HIGHEST, prefe...  5.05 us
    another operation x3, local copies, waits for them, and re-layouts  4.7 us
  transfers between devices with their start and end apart: 2, of which 2 were waited for; matrix products, arithmetic and copies ran while one was open for 2% of the time, Pallas kernels for 0%

commit v1 on v0

v1 whole, which is shorter than its diff:
```python
import jax
import jax.numpy as jnp
from jax import lax
from jax.experimental import pallas as pl
from jax.experimental.pallas import tpu as pltpu
from jax.sharding import PartitionSpec as P

CHIPS_Z = 8
GROUPS = 16
NB = 512
NARROW = 32
LANES = 128
PARTS = NB // LANES
STRIDE = 2 * PARTS


def split(x):
    high = x.astype(jnp.bfloat16)
    low = (x - high.astype(jnp.float32)).astype(jnp.bfloat16)
    return high, low


def product(left, right):
    def one(x, y):
        return jnp.dot(x, y, preferred_element_type=jnp.float32)

    return one(left[0], right[0]) + (one(left[0], right[1]) + one(left[1], right[0]))


def kernel(
    same_ref, other_ref, right_ref, inverse_ref, trailing_ref,
    updated_ref, own_ref,
    block, left_high, left_low, right_high, right_low, inv_high, inv_low, solved,
    in_sem, out_sem,
):
    row = lax.axis_index("prow")
    column = lax.axis_index("pcol")
    z, core = column // 2, column % 2
    beneath = row >= column
    fetch = pltpu.make_async_copy(trailing_ref, block, in_sem)
    fetch.start()

    inv_high[...], inv_low[...] = split(inverse_ref[...])
    for slot in range(CHIPS_Z):
        chip = lax.rem(z + CHIPS_Z - slot, CHIPS_Z)
        for source, where in ((same_ref, core), (other_ref, 1 - core)):
            rows = pl.ds(pl.multiple_of((chip * 2 + where) * NARROW, NARROW), NARROW)
            for a in range(2):
                left_high[a, rows, :], left_low[a, rows, :] = split(source[slot, a])
    for slot in range(GROUPS):
        rows = slice(slot * NARROW, (slot + 1) * NARROW)
        for b in range(2):
            right_high[b, rows, :], right_low[b, rows, :] = split(right_ref[slot, b])

    def solve(high, low):
        half = NB // 2
        upper = product(
            (inv_high[:half, :half], inv_low[:half, :half]),
            (high[:half, :], low[:half, :]),
        )
        lower = product((inv_high[half:, :], inv_low[half:, :]), (high[...], low[...]))
        return jnp.concatenate([upper, lower], 0)

    own_rows = pl.ds(pl.multiple_of(column * NARROW, NARROW), NARROW)
    for a in range(2):
        solved[...] = solve(left_high.at[a], left_low.at[a])
        own_ref[a] = solved[own_rows, :]
        left_high[a], left_low[a] = split(solved[...].T)
    for b in range(2):
        right_high[b], right_low[b] = split(solve(right_high.at[b], right_low.at[b]))
    fetch.wait()

    def lines(a, b, j):
        return pl.ds(a * NB * STRIDE + j * 2 + b, NB, stride=STRIDE)

    def update(a, b):
        change = product((left_high[a], left_low[a]), (right_high[b], right_low[b]))
        for j in range(PARTS):
            at = lines(a, b, j)
            block[at, :] = block[at, :] - change[:, j * LANES : (j + 1) * LANES]

    def clear(a, b):
        for j in range(PARTS):
            block[lines(a, b, j), :] = jnp.zeros((NB, LANES), jnp.float32)

    @pl.when(beneath)
    def _():
        update(0, 0)
        update(1, 1)

    @pl.when(jnp.logical_not(beneath))
    def _():
        clear(0, 0)
        clear(1, 1)

    clear(0, 1)
    update(1, 0)
    send = pltpu.make_async_copy(block, updated_ref, out_sem)
    send.start()
    send.wait()


def local(trailing, panel, diag_inverse):
    piece = panel.transpose(0, 2, 1)
    square = [(r * GROUPS + c, c * GROUPS + r) for r in range(GROUPS) for c in range(GROUPS)]
    turned = lax.ppermute(piece, ("prow", "pcol"), square)

    def around(step):
        return [(i, (i // 2 + step) % CHIPS_Z * 2 + i % 2) for i in range(GROUPS)]

    same = [piece] + [lax.ppermute(piece, "pcol", around(s)) for s in range(1, CHIPS_Z)]
    same = jnp.stack(same)
    other = lax.ppermute(same, "pcol", [(i, i ^ 1) for i in range(GROUPS)])
    right = lax.all_to_all(
        jnp.broadcast_to(turned[None], (GROUPS,) + turned.shape), "prow", 0, 0
    )
    view = trailing.reshape(2, NB, 2, PARTS, LANES).transpose(0, 1, 3, 2, 4)
    view = view.reshape(2 * NB * STRIDE, LANES)
    vmem = pl.BlockSpec(memory_space=pltpu.VMEM)
    hbm = pl.BlockSpec(memory_space=pl.ANY)
    half = pltpu.VMEM((2, NB, NB), jnp.bfloat16)
    updated, own = pl.pallas_call(
        kernel,
        out_shape=[
            jax.ShapeDtypeStruct(view.shape, jnp.float32),
            jax.ShapeDtypeStruct(piece.shape, jnp.float32),
        ],
        in_specs=[vmem, vmem, vmem, vmem, hbm],
        out_specs=[hbm, vmem],
        scratch_shapes=[
            pltpu.VMEM(view.shape, jnp.float32),
            half, half, half, half,
            pltpu.VMEM((NB, NB), jnp.bfloat16),
            pltpu.VMEM((NB, NB), jnp.bfloat16),
            pltpu.VMEM((NB, NB), jnp.float32),
            pltpu.SemaphoreType.DMA,
            pltpu.SemaphoreType.DMA,
        ],
        compiler_params=pltpu.CompilerParams(vmem_limit_bytes=48 * 1024 * 1024),
        name="update",
    )(same, other, right, diag_inverse, view)
    updated = updated.reshape(2, NB, PARTS, 2, LANES).transpose(0, 1, 3, 2, 4)
    return updated.reshape(trailing.shape), own.transpose(0, 2, 1)


def solution(mesh):
    return jax.shard_map(
        local,
        mesh=mesh,
        in_specs=(P(None, "prow", None, "pcol"), P(None, "prow", "pcol"), P()),
        out_specs=(P(None, "prow", None, "pcol"), P(None, "prow", "pcol")),
        check_vma=False,
    )
```

time: 207 us -> 96.5 us (0.47)
  the two profiles are of different devices: /device:TPU:6 before, /device:TPU:121 now
where the time goes in v1:
time: 96.5 us; the launch traced here: 96.1 us
  waiting for transfers between devices  46.3 us (48%)
  starting transfers between devices  29.3 us (30%)
  Pallas kernels  11 us (11%)
  local copies, waits for them, and re-layouts  8.73 us (9%)
    ppermute x1, waiting for transfers between devices, local(): turned = lax.ppermute(piece, ('prow', 'pcol'), square)  20.4 us
    ppermute x7, waiting for transfers between devices, local(): lax.ppermute(piece, 'pcol', around(s))  16.1 us
    all_to_all x1, starting transfers between devices, local(): lax.all_to_all(jnp.broadcast_to(turned[None], (GROUPS,) + turned.shape),...  16 us
    pallas_call x1, Pallas kernels, local(): pl.pallas_call(kernel, out_shape=[jax.ShapeDtypeStruct(view.shape, jnp.fl...  11 us
    ppermute x7, starting transfers between devices, local(): lax.ppermute(piece, 'pcol', around(s))  7.77 us
    all_to_all x1, waiting for transfers between devices, local(): lax.all_to_all(jnp.broadcast_to(turned[None], (GROUPS,) + turned.shape),...  7.53 us
    unnamed x15, local copies, waits for them, and re-layouts  7.14 us
    ppermute x1, starting transfers between devices, local(): turned = lax.ppermute(piece, ('prow', 'pcol'), square)  4.95 us
  transfers between devices with their start and end apart: 10, of which 5 were waited for; matrix products, arithmetic and copies ran while one was open for 6% of the time, Pallas kernels for 0%

profile of v1, /device:TPU:121, one launch (start us, length us, event | category | flops | bytes accessed | tf_op | source)
XLA Modules:
  0.0 96.1 jit_solution(15071724681593052148)
XLA Ops:
  0.6 0.0 copy-start.3
  0.6 0.1 collective-permute-start.6
  0.7 0.1 collective-permute-start.5
  0.8 5.6 %collective-permute-start.4 = (f32[2,32,512]{2,1,0:T(8,128)}, f32[2,32,512]{2,1,0:T(8,128)}, u32[]{:S(2)}, u32[]{:S(2)}) collective-permute-start(f32[2,32,512]{2,1,0:T(8,128)} %bitcast.32), channel_id=1, source_target_pairs={{0,10},{1,11},{2,12},{3,13},{4,14},{5,15},{6,0},{7,1},{8,2},{9,3},... | collective-permute-start | bytes 393224 | tf_op jit(solution)/shard_map/ppermute | solution.py:111
  6.4 1.9 %collective-permute-start = (f32[2,32,512]{2,1,0:T(8,128)}, f32[2,32,512]{2,1,0:T(8,128)}, u32[]{:S(2)}, u32[]{:S(2)}) collective-permute-start(f32[2,32,512]{2,1,0:T(8,128)} %bitcast.33), channel_id=1, source_target_pairs={{0,2},{1,3},{2,4},{3,5},{4,6},{5,7},{6,8},{7,9},{8,10},{9,11},{10,... | collective-permute-start | bytes 393224 | tf_op jit(solution)/shard_map/ppermute | solution.py:111
  8.3 4.9 %collective-permute-start.8 = (f32[2,32,512]{2,1,0:T(8,128)}, f32[2,32,512]{2,1,0:T(8,128)S(1)}, u32[]{:S(2)}, u32[]{:S(2)}) collective-permute-start(f32[2,32,512]{2,1,0:T(8,128)} %bitcast.34), channel_id=1, source_target_pairs={{0,0},{1,16},{2,32},{3,48},{4,64},{5,80},{6,96},{7,112},{8,128},{9... | collective-permute-start | bytes 393224 | tf_op jit(solution)/shard_map/ppermute | solution.py:106
  13.3 0.9 bitcast_dynamic-update-slice_fusion
  14.2 20.4 %collective-permute-done.8 = f32[2,32,512]{2,1,0:T(8,128)S(1)} collective-permute-done((f32[2,32,512]{2,1,0:T(8,128)}, f32[2,32,512]{2,1,0:T(8,128)S(1)}, u32[]{:S(2)}, u32[]{:S(2)}) %collective-permute-start.8) | collective-permute-done | bytes 131104 | tf_op jit(solution)/shard_map/ppermute | solution.py:106
  34.6 0.0 collective-permute-start.3
  34.6 1.6 %broadcast_in_dim.2 = f32[16,2,32,512]{3,2,1,0:T(8,128)} broadcast(f32[2,32,512]{2,1,0:T(8,128)S(1)} %collective-permute-done.8), dimensions={1,2,3} | broadcast | bytes 2228224 | tf_op jit(solution)/shard_map/broadcast_in_dim | solution.py:115
  36.2 16.0 %all-to-all-start = ((f32[16,2,32,512]{3,2,1,0:T(8,128)}), f32[16,2,32,512]{3,2,1,0:T(8,128)S(1)}, u32[]{:S(2)}, u32[]{:S(2)}) async-start(f32[16,2,32,512]{3,2,1,0:T(8,128)} %broadcast_in_dim.2), calls=%async_computation | async-start | bytes 4194304 | tf_op jit(solution)/shard_map/all_to_all | solution.py:114
  52.2 0.0 collective-permute-done
  52.2 0.0 copy-done.3
  52.2 0.1 collective-permute-start.1
  52.3 0.9 bitcast_dynamic-update-slice_fusion.7
  53.2 4.7 %collective-permute-done.1 = f32[2,32,512]{2,1,0:T(8,128)S(1)} collective-permute-done((f32[2,32,512]{2,1,0:T(8,128)S(1)}, f32[2,32,512]{2,1,0:T(8,128)S(1)}, u32[]{:S(2)}, u32[]{:S(2)}) %collective-permute-start.1) | collective-permute-done | bytes 131104 | tf_op jit(solution)/shard_map/ppermute | solution.py:111
  57.9 0.0 collective-permute-start.2
  58.0 11.4 %collective-permute-done.2 = f32[2,32,512]{2,1,0:T(8,128)S(1)} collective-permute-done((f32[2,32,512]{2,1,0:T(8,128)S(1)}, f32[2,32,512]{2,1,0:T(8,128)S(1)}, u32[]{:S(2)}, u32[]{:S(2)}) %collective-permute-start.2) | collective-permute-done | bytes 131104 | tf_op jit(solution)/shard_map/ppermute | solution.py:111
  69.4 0.0 collective-permute-done.3
  69.4 0.9 bitcast_dynamic-update-slice_fusion.4
  70.3 0.0 collective-permute-done.4
  70.3 0.9 bitcast_dynamic-update-slice_fusion.3
  71.2 0.0 collective-permute-done.5
  71.3 0.0 collective-permute-done.6
  71.3 0.6 collective-permute-start.7
  71.9 2.3 %collective-permute-done.7.other_ref = f32[8,2,32,512]{3,2,1,0:T(8,128)S(1)} collective-permute-done((f32[8,2,32,512]{3,2,1,0:T(8,128)S(1)}, f32[8,2,32,512]{3,2,1,0:T(8,128)S(1)}, u32[]{:S(2)}, u32[]{:S(2)}) %collective-permute-start.7) | collective-permute-done | bytes 1048608 | tf_op jit(solution)/shard_map/ppermute | solution.py:113
  74.2 0.0 copy-start.1
  74.2 1.0 %copy-done.1 = f32[8,2,32,512]{3,2,1,0:T(8,128)} copy-done((f32[8,2,32,512]{3,2,1,0:T(8,128)}, f32[8,2,32,512]{3,2,1,0:T(8,128)S(1)}, u32[]{:S(2)}) %copy-start.1) | copy-done | bytes 1048600
  75.2 7.5 %all-to-all-done.right_ref = f32[16,2,32,512]{3,2,1,0:T(8,128)S(1)} async-done(((f32[16,2,32,512]{3,2,1,0:T(8,128)}), f32[16,2,32,512]{3,2,1,0:T(8,128)S(1)}, u32[]{:S(2)}, u32[]{:S(2)}) %all-to-all-start) | async-done | bytes 2097184 | tf_op jit(solution)/shard_map/all_to_all | solution.py:114
  82.7 0.0 copy-start
  82.7 1.2 %copy-done = f32[512,512]{1,0:T(8,128)S(1)} copy-done((f32[512,512]{1,0:T(8,128)S(1)}, f32[512,512]{1,0:T(8,128)}, u32[]{:S(2)}) %copy-start) | copy-done | bytes 1048600
  83.9 0.0 copy-start.2
  83.9 1.2 %copy-done.2 = f32[8,2,32,512]{3,2,1,0:T(8,128)S(1)} copy-done((f32[8,2,32,512]{3,2,1,0:T(8,128)S(1)}, f32[8,2,32,512]{3,2,1,0:T(8,128)}, u32[]{:S(2)}) %copy-start.2) | copy-done | bytes 1048600
  85.1 11.0 %update.1 = (f32[8192,128]{1,0:T(8,128)}, f32[2,32,512]{2,1,0:T(8,128)}) custom-call(f32[8,2,32,512]{3,2,1,0:T(8,128)S(1)} %bitcast_dynamic-update-slice_fusion.1.same_ref, f32[8,2,32,512]{3,2,1,0:T(8,128)S(1)} %copy-done.2, f32[16,2,32,512]{3,2,1,0:T(8,128)S(1)} %all-to-all-done.right_ref, f32[512,512]{1,0:T(8,128)S(1)} %copy-done, f32[8192,128]{1,0:T(8,128)} %bitcast.29), custom_call_target="tpu_custom_call" | custom-call | tf_op jit(solution)/shard_map/update/pallas_call | solution.py:122
  (4 shorter events, 0.0 us)
Async XLA Ops:
  0.6 51.6 %copy-start.3 = (f32[2,512,32]{1,2,0:T(8,128)S(1)}, f32[2,512,32]{1,2,0:T(8,128)}, u32[]{:S(2)}) copy-start(f32[2,512,32]{1,2,0:T(8,128)} %param.4) | copy-start | bytes 393220
  0.6 70.6 %collective-permute-start.6 = (f32[2,32,512]{2,1,0:T(8,128)}, f32[2,32,512]{2,1,0:T(8,128)S(1)}, u32[]{:S(2)}, u32[]{:S(2)}) collective-permute-start(f32[2,32,512]{2,1,0:T(8,128)} %bitcast.30), channel_id=1, source_target_pairs={{0,14},{1,15},{2,0},{3,1},{4,2},{5,3},{6,4},{7,5},{8,6},{9,7},{10,... | collective-permute-start | bytes 393224 | tf_op jit(solution)/shard_map/ppermute | solution.py:111
  0.7 70.5 %collective-permute-start.5 = (f32[2,32,512]{2,1,0:T(8,128)}, f32[2,32,512]{2,1,0:T(8,128)S(1)}, u32[]{:S(2)}, u32[]{:S(2)}) collective-permute-start(f32[2,32,512]{2,1,0:T(8,128)} %bitcast.31), channel_id=1, source_target_pairs={{0,12},{1,13},{2,14},{3,15},{4,0},{5,1},{6,2},{7,3},{8,4},{9,5},{1... | collective-permute-start | bytes 393224 | tf_op jit(solution)/shard_map/ppermute | solution.py:111
  0.8 69.5 %collective-permute-start.4 = (f32[2,32,512]{2,1,0:T(8,128)}, f32[2,32,512]{2,1,0:T(8,128)}, u32[]{:S(2)}, u32[]{:S(2)}) collective-permute-start(f32[2,32,512]{2,1,0:T(8,128)} %bitcast.32), channel_id=1, source_target_pairs={{0,10},{1,11},{2,12},{3,13},{4,14},{5,15},{6,0},{7,1},{8,2},{9,3},... | collective-permute-start | bytes 393224 | tf_op jit(solution)/shard_map/ppermute | solution.py:111
  6.4 45.8 %collective-permute-start = (f32[2,32,512]{2,1,0:T(8,128)}, f32[2,32,512]{2,1,0:T(8,128)}, u32[]{:S(2)}, u32[]{:S(2)}) collective-permute-start(f32[2,32,512]{2,1,0:T(8,128)} %bitcast.33), channel_id=1, source_target_pairs={{0,2},{1,3},{2,4},{3,5},{4,6},{5,7},{6,8},{7,9},{8,10},{9,11},{10,... | collective-permute-start | bytes 393224 | tf_op jit(solution)/shard_map/ppermute | solution.py:111
  8.3 26.3 %collective-permute-start.8 = (f32[2,32,512]{2,1,0:T(8,128)}, f32[2,32,512]{2,1,0:T(8,128)S(1)}, u32[]{:S(2)}, u32[]{:S(2)}) collective-permute-start(f32[2,32,512]{2,1,0:T(8,128)} %bitcast.34), channel_id=1, source_target_pairs={{0,0},{1,16},{2,32},{3,48},{4,64},{5,80},{6,96},{7,112},{8,128},{9... | collective-permute-start | bytes 393224 | tf_op jit(solution)/shard_map/ppermute | solution.py:106
  34.6 34.8 %collective-permute-start.3 = (f32[2,32,512]{2,1,0:T(8,128)}, f32[2,32,512]{2,1,0:T(8,128)}, u32[]{:S(2)}, u32[]{:S(2)}) collective-permute-start(f32[2,32,512]{2,1,0:T(8,128)} %bitcast.35), channel_id=1, source_target_pairs={{0,8},{1,9},{2,10},{3,11},{4,12},{5,13},{6,14},{7,15},{8,0},{9,1},... | collective-permute-start | bytes 393224 | tf_op jit(solution)/shard_map/ppermute | solution.py:111
  36.2 46.5 %all-to-all-start = ((f32[16,2,32,512]{3,2,1,0:T(8,128)}), f32[16,2,32,512]{3,2,1,0:T(8,128)S(1)}, u32[]{:S(2)}, u32[]{:S(2)}) async-start(f32[16,2,32,512]{3,2,1,0:T(8,128)} %broadcast_in_dim.2), calls=%async_computation | async-start | bytes 4194304 | tf_op jit(solution)/shard_map/all_to_all | solution.py:114
  52.2 5.7 %collective-permute-start.1 = (f32[2,32,512]{2,1,0:T(8,128)S(1)}, f32[2,32,512]{2,1,0:T(8,128)S(1)}, u32[]{:S(2)}, u32[]{:S(2)}) collective-permute-start(f32[2,32,512]{2,1,0:T(8,128)S(1)} %bitcast.36), channel_id=1, source_target_pairs={{0,4},{1,5},{2,6},{3,7},{4,8},{5,9},{6,10},{7,11},{8,12},{9,13},{1... | collective-permute-start | bytes 393224 | tf_op jit(solution)/shard_map/ppermute | solution.py:111
  57.9 11.4 %collective-permute-start.2 = (f32[2,32,512]{2,1,0:T(8,128)S(1)}, f32[2,32,512]{2,1,0:T(8,128)S(1)}, u32[]{:S(2)}, u32[]{:S(2)}) collective-permute-start(f32[2,32,512]{2,1,0:T(8,128)S(1)} %bitcast.37), channel_id=1, source_target_pairs={{0,6},{1,7},{2,8},{3,9},{4,10},{5,11},{6,12},{7,13},{8,14},{9,15},... | collective-permute-start | bytes 393224 | tf_op jit(solution)/shard_map/ppermute | solution.py:111
  71.3 2.9 %collective-permute-start.7 = (f32[8,2,32,512]{3,2,1,0:T(8,128)S(1)}, f32[8,2,32,512]{3,2,1,0:T(8,128)S(1)}, u32[]{:S(2)}, u32[]{:S(2)}) collective-permute-start(f32[8,2,32,512]{3,2,1,0:T(8,128)S(1)} %bitcast_dynamic-update-slice_fusion.1.same_ref), channel_id=1, source_target_pairs={{0,1},{1,0},{2,3},{3,2},{4,5},{5,4},{6,7},{7,6},{8,9},{9,8},{10,11... | collective-permute-start | bytes 3145736 | tf_op jit(solution)/shard_map/ppermute | solution.py:113
  74.2 1.0 %copy-start.1 = (f32[8,2,32,512]{3,2,1,0:T(8,128)}, f32[8,2,32,512]{3,2,1,0:T(8,128)S(1)}, u32[]{:S(2)}) copy-start(f32[8,2,32,512]{3,2,1,0:T(8,128)S(1)} %collective-permute-done.7.other_ref) | copy-start | bytes 3145732
  82.7 1.2 %copy-start = (f32[512,512]{1,0:T(8,128)S(1)}, f32[512,512]{1,0:T(8,128)}, u32[]{:S(2)}) copy-start(f32[512,512]{1,0:T(8,128)} %inverse_ref.1) | copy-start | bytes 3145732
  83.9 1.2 %copy-start.2 = (f32[8,2,32,512]{3,2,1,0:T(8,128)S(1)}, f32[8,2,32,512]{3,2,1,0:T(8,128)}, u32[]{:S(2)}) copy-start(f32[8,2,32,512]{3,2,1,0:T(8,128)} %copy-done.1) | copy-start | bytes 3145732

commit v2 on v1

v2 whole, which is shorter than its diff:
```python
import functools

import jax
import jax.numpy as jnp
import numpy as np
from jax import lax
from jax.experimental import pallas as pl
from jax.experimental.pallas import tpu as pltpu
from jax.sharding import PartitionSpec as P

CHIPS_Z = 8
SIDE = 4
GROUPS = 16
NB = 512
HALF = NB // 2
NARROW = 32
LANES = 128
PARTS = NB // LANES
STRIDE = 2 * PARTS
OFFSETS = (0, -1, 1, 2)
PLACE = (
    (7, 14, 6, 2, 11, 9, 5, 8, 12, 1, 0, 4, 13, 15, 3, 10),
    (1, 12, 4, 15, 10, 7, 14, 3, 2, 0, 13, 6, 5, 8, 9, 11),
    (15, 6, 11, 9, 8, 4, 12, 0, 7, 13, 1, 14, 10, 3, 2, 5),
    (9, 13, 1, 0, 5, 10, 11, 3, 6, 4, 2, 15, 12, 7, 14, 8),
    (1, 3, 13, 14, 8, 5, 10, 15, 2, 6, 9, 7, 4, 0, 11, 12),
    (0, 14, 12, 7, 15, 2, 13, 11, 5, 3, 10, 8, 1, 4, 9, 6),
    (5, 4, 15, 2, 6, 0, 1, 12, 8, 14, 11, 13, 3, 9, 7, 10),
    (2, 8, 3, 6, 1, 9, 13, 14, 12, 15, 10, 0, 11, 5, 7, 4),
    (11, 12, 10, 0, 3, 1, 9, 4, 7, 14, 5, 2, 6, 15, 13, 8),
    (13, 8, 5, 9, 4, 11, 7, 15, 0, 10, 3, 2, 14, 12, 6, 1),
    (7, 15, 11, 10, 14, 13, 5, 2, 6, 9, 12, 8, 1, 0, 4, 3),
    (14, 9, 8, 15, 12, 7, 6, 0, 4, 1, 11, 3, 10, 13, 5, 2),
    (4, 5, 9, 12, 15, 0, 3, 1, 7, 13, 14, 10, 11, 8, 6, 2),
    (3, 10, 0, 1, 14, 12, 8, 2, 4, 5, 7, 9, 6, 15, 11, 13),
    (8, 2, 3, 13, 6, 1, 10, 15, 11, 9, 5, 12, 14, 7, 4, 0),
    (0, 5, 4, 7, 2, 13, 11, 14, 3, 10, 8, 6, 1, 9, 15, 12),
)
PIECE_AT = np.argsort(np.array(PLACE), axis=1).astype(np.int32)


def split(x):
    high = x.astype(jnp.bfloat16)
    low = (x - high.astype(jnp.float32)).astype(jnp.bfloat16)
    return high, low


def product(left, right):
    def one(x, y):
        return jnp.dot(x, y, preferred_element_type=jnp.float32)

    return one(left[0], right[0]) + (one(left[0], right[1]) + one(left[1], right[0]))


def chunk(index):
    return pl.ds(pl.multiple_of(index * NARROW, NARROW), NARROW)


def lines(a, b, j, start=0, count=NB):
    return pl.ds((a * NB + start) * STRIDE + j * 2 + b, count, stride=STRIDE)


def load_kernel(view_ref, piece_ref, inverse_ref, tiles_ref, kept_ref, high_ref, low_ref):
    kept_ref[...] = piece_ref[...]
    high_ref[...], low_ref[...] = split(inverse_ref[...])
    for a in range(2):
        for b in range(a + 1):
            for j in range(PARTS):
                tiles_ref[a + b, :, j * LANES : (j + 1) * LANES] = view_ref[lines(a, b, j), :]


def meet_kernel(count, *refs):
    outs = refs[len(refs) - count :]
    for source, to in zip(refs[:count], outs):
        to[...] = source[...]


def stack_kernel(counts, *refs):
    sources = iter(refs)
    outs = refs[sum(counts):]
    for count, out in zip(counts, outs):
        for slot in range(count):
            out[slot] = next(sources)[...]


def left_kernel(
    chips, other_ref, same_ref, other_four_ref, four_ref, inv_high, inv_low,
    high_ref, low_ref, own_ref,
    panel_high, panel_low, solved,
):
    column = lax.axis_index("pcol")
    z, core = column // 2, column % 2
    for slot, step in enumerate(chips):
        chip = lax.rem(z + CHIPS_Z - step, CHIPS_Z)
        far = slot == len(chips) - 1
        pair = (four_ref, other_four_ref) if far else (same_ref, other_ref)
        for source, where in zip(pair, (core, 1 - core)):
            rows = chunk(chip * 2 + where)
            for a in range(2):
                values = source[a] if far else source[slot, a]
                panel_high[a, rows, :], panel_low[a, rows, :] = split(values)
    for a in range(2):
        high, low = panel_high.at[a], panel_low.at[a]
        solved[:HALF, :] = product(
            (inv_high[:HALF, :HALF], inv_low[:HALF, :HALF]), (high[:HALF, :], low[:HALF, :])
        )
        solved[HALF:, :] = product(
            (inv_high[HALF:, :], inv_low[HALF:, :]), (high[...], low[...])
        )
        own_ref[a] = solved[chunk(column), :]
        high[...], low[...] = split(solved[...].T)
        high_ref[a, :, :HALF], low_ref[a, :, :HALF] = split(
            product((high[...], low[...]), (inv_high[:, :HALF], inv_low[:, :HALF]))
        )
        high_ref[a, :, HALF:], low_ref[a, :, HALF:] = split(
            product(
                (high[:, HALF:], low[:, HALF:]), (inv_high[HALF:, HALF:], inv_low[HALF:, HALF:])
            )
        )


def right_kernel(
    table_ref, second_ref, third_ref, fourth_ref, left_high, left_low, first_ref, tiles_ref,
    updated_ref,
    block, panel_high, panel_low, out_sem,
):
    row = lax.axis_index("prow")
    column = lax.axis_index("pcol")
    beneath = row >= column
    y, x, core = row // SIDE, row % SIDE, column % 2

    def place(b):
        for group, source in enumerate((first_ref, second_ref, third_ref, fourth_ref)):
            for slot in range(SIDE):
                to_y = jnp.where(core == 0, OFFSETS[group], OFFSETS[slot])
                to_x = jnp.where(core == 0, OFFSETS[slot], OFFSETS[group])
                at = lax.rem(y + to_y + SIDE, SIDE) * SIDE + lax.rem(x + to_x + SIDE, SIDE)
                rows = chunk(table_ref[column * GROUPS + at])
                panel_high[b, rows, :], panel_low[b, rows, :] = split(source[slot, b])

    def update(a, b, half):
        rows = slice(half * HALF, (half + 1) * HALF)
        change = product(
            (left_high[a, rows, :], left_low[a, rows, :]), (panel_high[b], panel_low[b])
        )
        result = tiles_ref[a + b, rows, :] - change
        for j in range(PARTS):
            block[lines(a, b, j, half * HALF, HALF), :] = result[:, j * LANES : (j + 1) * LANES]

    def clear(a, b, half):
        for j in range(PARTS):
            block[lines(a, b, j, half * HALF, HALF), :] = jnp.zeros((HALF, LANES), jnp.float32)

    def send(a, half):
        part = pl.ds((a * NB + half * HALF) * STRIDE, HALF * STRIDE)
        return pltpu.make_async_copy(
            block.at[part], updated_ref.at[part], out_sem.at[a * 2 + half]
        )

    place(0)
    for half in range(2):
        clear(0, 1, half)

        @pl.when(beneath)
        def _():
            update(0, 0, half)

        @pl.when(jnp.logical_not(beneath))
        def _():
            clear(0, 0, half)

        send(0, half).start()

    @pl.when(beneath)
    def _():
        place(1)

    for half in range(2):
        update(1, 0, half)

        @pl.when(beneath)
        def _():
            update(1, 1, half)

        @pl.when(jnp.logical_not(beneath))
        def _():
            clear(1, 1, half)

        send(1, half).start()
    for a in range(2):
        for half in range(2):
            send(a, half).wait()


VMEM = pl.BlockSpec(memory_space=pltpu.VMEM)
HBM = pl.BlockSpec(memory_space=pl.ANY)
SMEM = pl.BlockSpec(memory_space=pltpu.SMEM)


def params(mib):
    return pltpu.CompilerParams(vmem_limit_bytes=mib * 1024 * 1024)


def along_z(step):
    return [(i, (i // 2 + step) % CHIPS_Z * 2 + i % 2) for i in range(GROUPS)]


def in_plane(move, piece):
    pairs = []
    for r in range(GROUPS):
        for c in range(GROUPS):
            dy, dx = move if c % 2 == 0 else move[::-1]
            to = (r // SIDE + dy) % SIDE * SIDE + (r % SIDE + dx) % SIDE
            pairs.append((r * GROUPS + c, to * GROUPS + c))
    return lax.ppermute(piece, ("prow", "pcol"), pairs)


def cost(flops, elements):
    return pl.CostEstimate(flops=flops, transcendentals=0, bytes_accessed=4 * elements)


def like(*arrays):
    return [jax.ShapeDtypeStruct(a.shape, a.dtype) for a in arrays]


def meet(pieces, others=()):
    return pl.pallas_call(
        functools.partial(meet_kernel, len(pieces)),
        out_shape=like(*pieces),
        in_specs=[VMEM] * len(pieces) + [HBM] * len(others),
        out_specs=[VMEM] * len(pieces),
        compiler_params=params(4),
        cost_estimate=cost(0, 2 * sum(p.size for p in pieces)),
        name="meet",
    )(*pieces, *others)


def stacked(*groups):
    pieces = [p for group in groups for p in group]
    return pl.pallas_call(
        functools.partial(stack_kernel, [len(group) for group in groups]),
        out_shape=[
            jax.ShapeDtypeStruct((len(group),) + group[0].shape, jnp.float32)
            for group in groups
        ],
        in_specs=[VMEM] * len(pieces),
        out_specs=[VMEM] * len(groups),
        compiler_params=params(4),
        cost_estimate=cost(0, 2 * sum(p.size for p in pieces)),
        name="stack",
    )(*pieces)


def local(trailing, panel, diag_inverse):
    piece = panel.transpose(0, 2, 1)
    view = trailing.reshape(2, NB, 2, PARTS, LANES).transpose(0, 1, 3, 2, 4)
    view = view.reshape(2 * NB * STRIDE, LANES)
    whole = jax.ShapeDtypeStruct((NB, NB), jnp.bfloat16)
    pair = jax.ShapeDtypeStruct((2, NB, NB), jnp.bfloat16)

    def by(step, block):
        return lax.ppermute(block, "pcol", along_z(step))

    def swap(block):
        return lax.ppermute(block, "pcol", [(i, i ^ 1) for i in range(GROUPS)])

    tiles, kept, inv_high, inv_low = pl.pallas_call(
        load_kernel,
        out_shape=[jax.ShapeDtypeStruct((3, NB, NB), jnp.float32), *like(piece), whole, whole],
        in_specs=[VMEM] * 3,
        out_specs=[VMEM] * 4,
        compiler_params=params(12),
        cost_estimate=cost(0, 8 * NB * NB),
        name="load",
    )(view, piece, diag_inverse)

    one, seven = by(1, piece), by(-1, piece)
    two, six = by(1, one), by(-1, seven)
    turn = [
        (r * GROUPS + c, PLACE[r][c] * GROUPS + r)
        for r in range(GROUPS)
        for c in range(GROUPS)
    ]
    turned = lax.ppermute(piece, ("prow", "pcol"), turn)
    one, seven, two, six, turned = meet([one, seven, two, six, turned], [tiles])

    three, five = by(1, two), by(-1, six)
    planar = [in_plane(m, turned) for m in ((0, 1), (0, -1), (0, 2))]
    same, first = stacked([kept, one, seven, two, six, three, five], [turned] + planar)

    four = by(1, same[5])
    other, other_four = swap(same), swap(four)
    rest = [in_plane(m, first) for m in ((1, 0), (-1, 0), (2, 0))]
    left_high, left_low, own = pl.pallas_call(
        functools.partial(left_kernel, (0, 1, 7, 2, 6, 3, 5, 4)),
        out_shape=[pair, pair, *like(piece)],
        in_specs=[VMEM] * 6,
        out_specs=[VMEM] * 3,
        scratch_shapes=[
            pltpu.VMEM(pair.shape, pair.dtype),
            pltpu.VMEM(pair.shape, pair.dtype),
            pltpu.VMEM((NB, NB), jnp.float32),
        ],
        compiler_params=params(16),
        cost_estimate=cost(20 * NB**3, 6 * NB * NB),
        name="left",
    )(other, same, other_four, four, inv_high, inv_low)

    updated = pl.pallas_call(
        right_kernel,
        out_shape=jax.ShapeDtypeStruct(view.shape, jnp.float32),
        in_specs=[SMEM] + [VMEM] * 7,
        out_specs=HBM,
        scratch_shapes=[
            pltpu.VMEM(view.shape, jnp.float32),
            pltpu.VMEM(pair.shape, pair.dtype),
            pltpu.VMEM(pair.shape, pair.dtype),
            pltpu.SemaphoreType.DMA((4,)),
        ],
        compiler_params=params(16),
        cost_estimate=cost(18 * NB**3, 12 * NB * NB),
        name="right",
    )(jnp.asarray(PIECE_AT.reshape(-1)), *rest, left_high, left_low, first, tiles)
    updated = updated.reshape(2, NB, PARTS, 2, LANES).transpose(0, 1, 3, 2, 4)
    return updated.reshape(trailing.shape), own.transpose(0, 2, 1)


def solution(mesh):
    return jax.shard_map(
        local,
        mesh=mesh,
        in_specs=(P(None, "prow", None, "pcol"), P(None, "prow", "pcol"), P()),
        out_specs=(P(None, "prow", None, "pcol"), P(None, "prow", "pcol")),
        check_vma=False,
    )
```

time: 96.5 us -> 62.6 us (0.65)
  the two profiles are of different devices: /device:TPU:121 before, /device:TPU:1 now
where the time goes in v2:
time: 62.6 us; the launch traced here: 62.4 us
  starting transfers between devices  27.3 us (44%)
  waiting for transfers between devices  22 us (35%)
  Pallas kernels  7.95 us (13%)
  local copies, waits for them, and re-layouts  4.33 us (7%)
  between operations  0.87 us (1%)
    ppermute x7, waiting for transfers between devices, by(): return lax.ppermute(block, 'pcol', along_z(step))  12.8 us
    ppermute x7, starting transfers between devices, by(): return lax.ppermute(block, 'pcol', along_z(step))  11.9 us
    ppermute x2, starting transfers between devices, swap(): return lax.ppermute(block, 'pcol', [(i, i ^ 1) for i in range(GROUPS)])  6.43 us
    ppermute x6, waiting for transfers between devices, in_plane(): return lax.ppermute(piece, ('prow', 'pcol'), pairs)  6.27 us
    ppermute x1, starting transfers between devices, local(): turned = lax.ppermute(piece, ('prow', 'pcol'), turn)  6.04 us
    unnamed x8, local copies, waits for them, and re-layouts  4.32 us
    pallas_call x1, Pallas kernels, local(): pl.pallas_call(right_kernel, out_shape=jax.ShapeDtypeStruct(view.shape, j...  3.71 us
    pallas_call x1, Pallas kernels, local(): pl.pallas_call(functools.partial(left_kernel, (0, 1, 7, 2, 6, 3, 5, 4)),...  3.28 us
  transfers between devices with their start and end apart: 16, of which 9 were waited for; matrix products, arithmetic and copies ran while one was open for 0% of the time, Pallas kernels for 7%

profile of v2, /device:TPU:1, one launch (start us, length us, event | category | flops | bytes accessed | tf_op | source)
XLA Modules:
  0.0 62.4 jit_solution(13755486891592907817)
XLA Ops:
  0.6 6.5 %collective-permute-start.1 = (f32[2,32,512]{2,1,0:T(8,128)}, f32[2,32,512]{2,1,0:T(8,128)S(1)}, u32[]{:S(2)}, u32[]{:S(2)}) collective-permute-start(f32[2,32,512]{2,1,0:T(8,128)} %bitcast.15), channel_id=1, source_target_pairs={{0,14},{1,15},{2,0},{3,1},{4,2},{5,3},{6,4},{7,5},{8,6},{9,7},{10,... | collective-permute-start | bytes 393224 | tf_op jit(solution)/shard_map/ppermute | solution.py:262
  7.1 0.0 collective-permute-start
  7.1 6.0 %collective-permute-start.4 = (f32[2,32,512]{2,1,0:T(8,128)}, f32[2,32,512]{2,1,0:T(8,128)S(1)}, u32[]{:S(2)}, u32[]{:S(2)}) collective-permute-start(f32[2,32,512]{2,1,0:T(8,128)} %bitcast.17), channel_id=1, source_target_pairs={{0,112},{1,224},{2,96},{3,32},{4,176},{5,144},{6,80},{7,128},{8,19... | collective-permute-start | bytes 393224 | tf_op jit(solution)/shard_map/ppermute | solution.py:284
  13.2 0.0 collective-permute-done.1.refs_1_
  13.2 2.6 %collective-permute-start.3 = (f32[2,32,512]{2,1,0:T(8,128)S(1)}, f32[2,32,512]{2,1,0:T(8,128)S(1)}, u32[]{:S(2)}, u32[]{:S(2)}) collective-permute-start(f32[2,32,512]{2,1,0:T(8,128)S(1)} %collective-permute-done.1.refs_1_), channel_id=1, source_target_pairs={{0,14},{1,15},{2,0},{3,1},{4,2},{5,3},{6,4},{7,5},{8,6},{9,7},{10,... | collective-permute-start | bytes 393224 | tf_op jit(solution)/shard_map/ppermute | solution.py:262
  15.7 0.0 collective-permute-done.refs_0_
  15.7 0.0 collective-permute-start.2
  15.7 0.0 copy-start
  15.7 2.2 %copy-done = f32[2,512,2,512]{3,2,1,0:T(2,128)S(1)} copy-done((f32[2,512,2,512]{3,2,1,0:T(2,128)S(1)}, f32[2,512,2,512]{3,2,1,0:T(2,128)}, u32[]{:S(2)}) %copy-start) | copy-done | bytes 4194328
  17.9 0.0 copy-start.1
  17.9 1.2 %copy-done.1 = f32[512,512]{1,0:T(8,128)S(1)} copy-done((f32[512,512]{1,0:T(8,128)S(1)}, f32[512,512]{1,0:T(8,128)}, u32[]{:S(2)}) %copy-start.1) | copy-done | bytes 1048600
  19.1 0.0 copy-start.2
  19.2 0.9 %copy-done.2 = f32[2,512,32]{1,2,0:T(8,128)S(1)} copy-done((f32[2,512,32]{1,2,0:T(8,128)S(1)}, f32[2,512,32]{1,2,0:T(8,128)}, u32[]{:S(2)}) %copy-start.2) | copy-done | bytes 131096
  20.1 0.8 %load.1 = (f32[3,512,512]{2,1,0:T(8,128)S(1)}, f32[2,32,512]{2,1,0:T(8,128)S(1)}, bf16[512,512]{1,0:T(8,128)(2,1)S(1)}, bf16[512,512]{1,0:T(8,128)(2,1)S(1)}) custom-call(f32[8192,128]{1,0:T(8,128)S(1)} %bitcast.14, f32[2,32,512]{2,1,0:T(8,128)S(1)} %bitcast.18, f32[512,512]{1,0:T(8,128)S(1)} %copy-done.1), custom_call_target="tpu_custom_call" | custom-call | bytes 8388608 | tf_op jit(solution)/shard_map/load/pallas_call | solution.py:267
  20.9 2.0 %collective-permute-done.4.refs_4_ = f32[2,32,512]{2,1,0:T(8,128)S(1)} collective-permute-done((f32[2,32,512]{2,1,0:T(8,128)}, f32[2,32,512]{2,1,0:T(8,128)S(1)}, u32[]{:S(2)}, u32[]{:S(2)}) %collective-permute-start.4) | collective-permute-done | bytes 131104 | tf_op jit(solution)/shard_map/ppermute | solution.py:284
  22.9 0.8 %collective-permute-done.3.refs_3_ = f32[2,32,512]{2,1,0:T(8,128)S(1)} collective-permute-done((f32[2,32,512]{2,1,0:T(8,128)S(1)}, f32[2,32,512]{2,1,0:T(8,128)S(1)}, u32[]{:S(2)}, u32[]{:S(2)}) %collective-permute-start.3) | collective-permute-done | bytes 131104 | tf_op jit(solution)/shard_map/ppermute | solution.py:262
  23.7 4.7 %collective-permute-done.2.refs_2_ = f32[2,32,512]{2,1,0:T(8,128)S(1)} collective-permute-done((f32[2,32,512]{2,1,0:T(8,128)S(1)}, f32[2,32,512]{2,1,0:T(8,128)S(1)}, u32[]{:S(2)}, u32[]{:S(2)}) %collective-permute-start.2) | collective-permute-done | bytes 131104 | tf_op jit(solution)/shard_map/ppermute | solution.py:262
  28.5 0.1 collective-permute-start.5
  28.5 2.7 %collective-permute-start.6 = (f32[2,32,512]{2,1,0:T(8,128)S(1)}, f32[2,32,512]{2,1,0:T(8,128)S(1)}, u32[]{:S(2)}, u32[]{:S(2)}) collective-permute-start(f32[2,32,512]{2,1,0:T(8,128)S(1)} %get-tuple-element.21.refs_4_), channel_id=1, source_target_pairs={{0,14},{1,15},{2,0},{3,1},{4,2},{5,3},{6,4},{7,5},{8,6},{9,7},{10,... | collective-permute-start | bytes 393224 | tf_op jit(solution)/shard_map/ppermute | solution.py:262
  31.2 0.0 collective-permute-start.9
  31.2 0.7 %collective-permute-start.8 = (f32[2,32,512]{2,1,0:T(8,128)S(1)}, f32[2,32,512]{2,1,0:T(8,128)S(1)}, u32[]{:S(2)}, u32[]{:S(2)}) collective-permute-start(f32[2,32,512]{2,1,0:T(8,128)S(1)} %get-tuple-element.22.refs_7_), channel_id=1, source_target_pairs={{0,48},{1,193},{2,50},{3,195},{4,52},{5,197},{6,54},{7,199},{8,56}... | collective-permute-start | bytes 393224 | tf_op jit(solution)/shard_map/ppermute | solution.py:215
  31.9 0.8 %collective-permute-start.7 = (f32[2,32,512]{2,1,0:T(8,128)S(1)}, f32[2,32,512]{2,1,0:T(8,128)S(1)}, u32[]{:S(2)}, u32[]{:S(2)}) collective-permute-start(f32[2,32,512]{2,1,0:T(8,128)S(1)} %get-tuple-element.22.refs_7_), channel_id=1, source_target_pairs={{0,16},{1,65},{2,18},{3,67},{4,20},{5,69},{6,22},{7,71},{8,24},{9,... | collective-permute-start | bytes 393224 | tf_op jit(solution)/shard_map/ppermute | solution.py:215
  32.7 1.7 %collective-permute-done.5.refs_5_ = f32[2,32,512]{2,1,0:T(8,128)S(1)} collective-permute-done((f32[2,32,512]{2,1,0:T(8,128)S(1)}, f32[2,32,512]{2,1,0:T(8,128)S(1)}, u32[]{:S(2)}, u32[]{:S(2)}) %collective-permute-start.5) | collective-permute-done | bytes 131104 | tf_op jit(solution)/shard_map/ppermute | solution.py:262
  34.4 0.0 collective-permute-done.6.refs_6_
  34.4 2.2 %collective-permute-done.9.refs_10_ = f32[2,32,512]{2,1,0:T(8,128)S(1)} collective-permute-done((f32[2,32,512]{2,1,0:T(8,128)S(1)}, f32[2,32,512]{2,1,0:T(8,128)S(1)}, u32[]{:S(2)}, u32[]{:S(2)}) %collective-permute-start.9) | collective-permute-done | bytes 131104 | tf_op jit(solution)/shard_map/ppermute | solution.py:215
  36.6 0.0 collective-permute-done.8.refs_9_
  36.6 1.6 %collective-permute-done.7.refs_8_ = f32[2,32,512]{2,1,0:T(8,128)S(1)} collective-permute-done((f32[2,32,512]{2,1,0:T(8,128)S(1)}, f32[2,32,512]{2,1,0:T(8,128)S(1)}, u32[]{:S(2)}, u32[]{:S(2)}) %collective-permute-start.7) | collective-permute-done | bytes 131104 | tf_op jit(solution)/shard_map/ppermute | solution.py:215
  38.2 0.1 stack.1
  38.3 4.8 %collective-permute-start.13 = (f32[7,2,32,512]{3,2,1,0:T(8,128)S(1)}, f32[7,2,32,512]{3,2,1,0:T(8,128)S(1)}, u32[]{:S(2)}, u32[]{:S(2)}) collective-permute-start(f32[7,2,32,512]{3,2,1,0:T(8,128)S(1)} %get-tuple-element.24.same_ref), channel_id=1, source_target_pairs={{0,1},{1,0},{2,3},{3,2},{4,5},{5,4},{6,7},{7,6},{8,9},{9,8},{10,11... | collective-permute-start | bytes 2752520 | tf_op jit(solution)/shard_map/ppermute | solution.py:265
  43.1 0.0 collective-permute-start.12
  43.1 0.9 %collective-permute-start.11 = (f32[4,2,32,512]{3,2,1,0:T(8,128)S(1)}, f32[4,2,32,512]{3,2,1,0:T(8,128)S(1)}, u32[]{:S(2)}, u32[]{:S(2)}) collective-permute-start(f32[4,2,32,512]{3,2,1,0:T(8,128)S(1)} %get-tuple-element.23.first_ref), channel_id=1, source_target_pairs={{0,192},{1,49},{2,194},{3,51},{4,196},{5,53},{6,198},{7,55},{8,200... | collective-permute-start | bytes 1572872 | tf_op jit(solution)/shard_map/ppermute | solution.py:215
  44.0 0.6 collective-permute-start.10
  44.6 0.1 collective-permute-start.14
  44.7 5.5 %collective-permute-done.14.four_ref = f32[2,32,512]{2,1,0:T(8,128)S(1)} collective-permute-done((f32[2,32,512]{2,1,0:T(8,128)S(1)}, f32[2,32,512]{2,1,0:T(8,128)S(1)}, u32[]{:S(2)}, u32[]{:S(2)}) %collective-permute-start.14) | collective-permute-done | bytes 131104 | tf_op jit(solution)/shard_map/ppermute | solution.py:262
  50.2 1.6 %collective-permute-start.15 = (f32[2,32,512]{2,1,0:T(8,128)S(1)}, f32[2,32,512]{2,1,0:T(8,128)S(1)}, u32[]{:S(2)}, u32[]{:S(2)}) collective-permute-start(f32[2,32,512]{2,1,0:T(8,128)S(1)} %collective-permute-done.14.four_ref), channel_id=1, source_target_pairs={{0,1},{1,0},{2,3},{3,2},{4,5},{5,4},{6,7},{7,6},{8,9},{9,8},{10,11... | collective-permute-start | bytes 393224 | tf_op jit(solution)/shard_map/ppermute | solution.py:265
  51.8 1.0 %collective-permute-done.15.other_four_ref = f32[2,32,512]{2,1,0:T(8,128)S(1)} collective-permute-done((f32[2,32,512]{2,1,0:T(8,128)S(1)}, f32[2,32,512]{2,1,0:T(8,128)S(1)}, u32[]{:S(2)}, u32[]{:S(2)}) %collective-permute-start.15) | collective-permute-done | bytes 131104 | tf_op jit(solution)/shard_map/ppermute | solution.py:265
  52.8 0.0 collective-permute-done.13.other_ref
  52.8 0.0 copy-start.3
  52.8 3.3 %left.1 = (bf16[2,512,512]{2,1,0:T(8,128)(2,1)S(1)}, bf16[2,512,512]{2,1,0:T(8,128)(2,1)S(1)}, f32[2,32,512]{2,1,0:T(8,128)}) custom-call(f32[7,2,32,512]{3,2,1,0:T(8,128)S(1)} %collective-permute-done.13.other_ref, f32[7,2,32,512]{3,2,1,0:T(8,128)S(1)} %get-tuple-element.24.same_ref, f32[2,32,512]{2,1,0:T(8,128)S(1)} %collective-permute-done.15.other_four_ref, ...), custom_call_target="tpu_custom_call" | custom-call | flops 2684354560 | bytes 6291456 | tf_op jit(solution)/shard_map/left/pallas_call | solution.py:294
  56.1 0.0 collective-permute-done.12.fourth_ref
  56.1 0.0 collective-permute-done.11.third_ref
  56.1 2.5 %collective-permute-done.10.second_ref = f32[4,2,32,512]{3,2,1,0:T(8,128)S(1)} collective-permute-done((f32[4,2,32,512]{3,2,1,0:T(8,128)S(1)}, f32[4,2,32,512]{3,2,1,0:T(8,128)S(1)}, u32[]{:S(2)}, u32[]{:S(2)}) %collective-permute-start.10) | collective-permute-done | bytes 524320 | tf_op jit(solution)/shard_map/ppermute | solution.py:215
  58.6 0.0 copy-done.3
  58.6 3.7 %right.1 = f32[8192,128]{1,0:T(8,128)} custom-call(s32[256]{0:T(256)S(1)} %copy-done.3, f32[4,2,32,512]{3,2,1,0:T(8,128)S(1)} %collective-permute-done.10.second_ref, f32[4,2,32,512]{3,2,1,0:T(8,128)S(1)} %collective-permute-done.11.third_ref, f32[4,2,32,512]{3,2,1,0:T(8,128)S(1)} %collective-permute-done.12.fourth_ref, ...), custom_call_target="tpu_custom_call" | custom-call | flops 2415919104 | bytes 12582912 | tf_op jit(solution)/shard_map/right/pallas_call | solution.py:309
  (2 shorter events, 0.1 us)
Async XLA Ops:
  0.6 12.5 %collective-permute-start.1 = (f32[2,32,512]{2,1,0:T(8,128)}, f32[2,32,512]{2,1,0:T(8,128)S(1)}, u32[]{:S(2)}, u32[]{:S(2)}) collective-permute-start(f32[2,32,512]{2,1,0:T(8,128)} %bitcast.15), channel_id=1, source_target_pairs={{0,14},{1,15},{2,0},{3,1},{4,2},{5,3},{6,4},{7,5},{8,6},{9,7},{10,... | collective-permute-start | bytes 393224 | tf_op jit(solution)/shard_map/ppermute | solution.py:262
  7.1 8.6 %collective-permute-start = (f32[2,32,512]{2,1,0:T(8,128)}, f32[2,32,512]{2,1,0:T(8,128)S(1)}, u32[]{:S(2)}, u32[]{:S(2)}) collective-permute-start(f32[2,32,512]{2,1,0:T(8,128)} %bitcast.16), channel_id=1, source_target_pairs={{0,2},{1,3},{2,4},{3,5},{4,6},{5,7},{6,8},{7,9},{8,10},{9,11},{10,... | collective-permute-start | bytes 393224 | tf_op jit(solution)/shard_map/ppermute | solution.py:262
  7.1 15.8 %collective-permute-start.4 = (f32[2,32,512]{2,1,0:T(8,128)}, f32[2,32,512]{2,1,0:T(8,128)S(1)}, u32[]{:S(2)}, u32[]{:S(2)}) collective-permute-start(f32[2,32,512]{2,1,0:T(8,128)} %bitcast.17), channel_id=1, source_target_pairs={{0,112},{1,224},{2,96},{3,32},{4,176},{5,144},{6,80},{7,128},{8,19... | collective-permute-start | bytes 393224 | tf_op jit(solution)/shard_map/ppermute | solution.py:284
  13.2 10.5 %collective-permute-start.3 = (f32[2,32,512]{2,1,0:T(8,128)S(1)}, f32[2,32,512]{2,1,0:T(8,128)S(1)}, u32[]{:S(2)}, u32[]{:S(2)}) collective-permute-start(f32[2,32,512]{2,1,0:T(8,128)S(1)} %collective-permute-done.1.refs_1_), channel_id=1, source_target_pairs={{0,14},{1,15},{2,0},{3,1},{4,2},{5,3},{6,4},{7,5},{8,6},{9,7},{10,... | collective-permute-start | bytes 393224 | tf_op jit(solution)/shard_map/ppermute | solution.py:262
  15.7 12.7 %collective-permute-start.2 = (f32[2,32,512]{2,1,0:T(8,128)S(1)}, f32[2,32,512]{2,1,0:T(8,128)S(1)}, u32[]{:S(2)}, u32[]{:S(2)}) collective-permute-start(f32[2,32,512]{2,1,0:T(8,128)S(1)} %collective-permute-done.refs_0_), channel_id=1, source_target_pairs={{0,2},{1,3},{2,4},{3,5},{4,6},{5,7},{6,8},{7,9},{8,10},{9,11},{10,... | collective-permute-start | bytes 393224 | tf_op jit(solution)/shard_map/ppermute | solution.py:262
  15.7 2.2 %copy-start = (f32[2,512,2,512]{3,2,1,0:T(2,128)S(1)}, f32[2,512,2,512]{3,2,1,0:T(2,128)}, u32[]{:S(2)}) copy-start(f32[2,512,2,512]{3,2,1,0:T(2,128)} %param.4) | copy-start | bytes 12582916
  17.9 1.2 %copy-start.1 = (f32[512,512]{1,0:T(8,128)S(1)}, f32[512,512]{1,0:T(8,128)}, u32[]{:S(2)}) copy-start(f32[512,512]{1,0:T(8,128)} %inverse_ref.1) | copy-start | bytes 3145732
  19.1 0.9 %copy-start.2 = (f32[2,512,32]{1,2,0:T(8,128)S(1)}, f32[2,512,32]{1,2,0:T(8,128)}, u32[]{:S(2)}) copy-start(f32[2,512,32]{1,2,0:T(8,128)} %param.5) | copy-start | bytes 393220
  28.5 6.0 %collective-permute-start.5 = (f32[2,32,512]{2,1,0:T(8,128)S(1)}, f32[2,32,512]{2,1,0:T(8,128)S(1)}, u32[]{:S(2)}, u32[]{:S(2)}) collective-permute-start(f32[2,32,512]{2,1,0:T(8,128)S(1)} %get-tuple-element.20.refs_3_), channel_id=1, source_target_pairs={{0,2},{1,3},{2,4},{3,5},{4,6},{5,7},{6,8},{7,9},{8,10},{9,11},{10,... | collective-permute-start | bytes 393224 | tf_op jit(solution)/shard_map/ppermute | solution.py:262
  28.5 5.9 %collective-permute-start.6 = (f32[2,32,512]{2,1,0:T(8,128)S(1)}, f32[2,32,512]{2,1,0:T(8,128)S(1)}, u32[]{:S(2)}, u32[]{:S(2)}) collective-permute-start(f32[2,32,512]{2,1,0:T(8,128)S(1)} %get-tuple-element.21.refs_4_), channel_id=1, source_target_pairs={{0,14},{1,15},{2,0},{3,1},{4,2},{5,3},{6,4},{7,5},{8,6},{9,7},{10,... | collective-permute-start | bytes 393224 | tf_op jit(solution)/shard_map/ppermute | solution.py:262
  31.2 5.4 %collective-permute-start.9 = (f32[2,32,512]{2,1,0:T(8,128)S(1)}, f32[2,32,512]{2,1,0:T(8,128)S(1)}, u32[]{:S(2)}, u32[]{:S(2)}) collective-permute-start(f32[2,32,512]{2,1,0:T(8,128)S(1)} %get-tuple-element.22.refs_7_), channel_id=1, source_target_pairs={{0,32},{1,129},{2,34},{3,131},{4,36},{5,133},{6,38},{7,135},{8,40}... | collective-permute-start | bytes 393224 | tf_op jit(solution)/shard_map/ppermute | solution.py:215
  31.2 5.4 %collective-permute-start.8 = (f32[2,32,512]{2,1,0:T(8,128)S(1)}, f32[2,32,512]{2,1,0:T(8,128)S(1)}, u32[]{:S(2)}, u32[]{:S(2)}) collective-permute-start(f32[2,32,512]{2,1,0:T(8,128)S(1)} %get-tuple-element.22.refs_7_), channel_id=1, source_target_pairs={{0,48},{1,193},{2,50},{3,195},{4,52},{5,197},{6,54},{7,199},{8,56}... | collective-permute-start | bytes 393224 | tf_op jit(solution)/shard_map/ppermute | solution.py:215
  31.9 6.3 %collective-permute-start.7 = (f32[2,32,512]{2,1,0:T(8,128)S(1)}, f32[2,32,512]{2,1,0:T(8,128)S(1)}, u32[]{:S(2)}, u32[]{:S(2)}) collective-permute-start(f32[2,32,512]{2,1,0:T(8,128)S(1)} %get-tuple-element.22.refs_7_), channel_id=1, source_target_pairs={{0,16},{1,65},{2,18},{3,67},{4,20},{5,69},{6,22},{7,71},{8,24},{9,... | collective-permute-start | bytes 393224 | tf_op jit(solution)/shard_map/ppermute | solution.py:215
  38.3 14.5 %collective-permute-start.13 = (f32[7,2,32,512]{3,2,1,0:T(8,128)S(1)}, f32[7,2,32,512]{3,2,1,0:T(8,128)S(1)}, u32[]{:S(2)}, u32[]{:S(2)}) collective-permute-start(f32[7,2,32,512]{3,2,1,0:T(8,128)S(1)} %get-tuple-element.24.same_ref), channel_id=1, source_target_pairs={{0,1},{1,0},{2,3},{3,2},{4,5},{5,4},{6,7},{7,6},{8,9},{9,8},{10,11... | collective-permute-start | bytes 2752520 | tf_op jit(solution)/shard_map/ppermute | solution.py:265
  43.1 13.0 %collective-permute-start.12 = (f32[4,2,32,512]{3,2,1,0:T(8,128)S(1)}, f32[4,2,32,512]{3,2,1,0:T(8,128)S(1)}, u32[]{:S(2)}, u32[]{:S(2)}) collective-permute-start(f32[4,2,32,512]{3,2,1,0:T(8,128)S(1)} %get-tuple-element.23.first_ref), channel_id=1, source_target_pairs={{0,128},{1,33},{2,130},{3,35},{4,132},{5,37},{6,134},{7,39},{8,136... | collective-permute-start | bytes 1572872 | tf_op jit(solution)/shard_map/ppermute | solution.py:215
  43.1 13.0 %collective-permute-start.11 = (f32[4,2,32,512]{3,2,1,0:T(8,128)S(1)}, f32[4,2,32,512]{3,2,1,0:T(8,128)S(1)}, u32[]{:S(2)}, u32[]{:S(2)}) collective-permute-start(f32[4,2,32,512]{3,2,1,0:T(8,128)S(1)} %get-tuple-element.23.first_ref), channel_id=1, source_target_pairs={{0,192},{1,49},{2,194},{3,51},{4,196},{5,53},{6,198},{7,55},{8,200... | collective-permute-start | bytes 1572872 | tf_op jit(solution)/shard_map/ppermute | solution.py:215
  44.0 14.5 %collective-permute-start.10 = (f32[4,2,32,512]{3,2,1,0:T(8,128)S(1)}, f32[4,2,32,512]{3,2,1,0:T(8,128)S(1)}, u32[]{:S(2)}, u32[]{:S(2)}) collective-permute-start(f32[4,2,32,512]{3,2,1,0:T(8,128)S(1)} %get-tuple-element.23.first_ref), channel_id=1, source_target_pairs={{0,64},{1,17},{2,66},{3,19},{4,68},{5,21},{6,70},{7,23},{8,72},{9,... | collective-permute-start | bytes 1572872 | tf_op jit(solution)/shard_map/ppermute | solution.py:215
  44.6 5.6 %collective-permute-start.14 = (f32[2,32,512]{2,1,0:T(8,128)S(1)}, f32[2,32,512]{2,1,0:T(8,128)S(1)}, u32[]{:S(2)}, u32[]{:S(2)}) collective-permute-start(f32[2,32,512]{2,1,0:T(8,128)S(1)} %slice_bitcast_fusion), channel_id=1, source_target_pairs={{0,2},{1,3},{2,4},{3,5},{4,6},{5,7},{6,8},{7,9},{8,10},{9,11},{10,... | collective-permute-start | bytes 393224 | tf_op jit(solution)/shard_map/ppermute | solution.py:262
  50.2 2.6 %collective-permute-start.15 = (f32[2,32,512]{2,1,0:T(8,128)S(1)}, f32[2,32,512]{2,1,0:T(8,128)S(1)}, u32[]{:S(2)}, u32[]{:S(2)}) collective-permute-start(f32[2,32,512]{2,1,0:T(8,128)S(1)} %collective-permute-done.14.four_ref), channel_id=1, source_target_pairs={{0,1},{1,0},{2,3},{3,2},{4,5},{5,4},{6,7},{7,6},{8,9},{9,8},{10,11... | collective-permute-start | bytes 393224 | tf_op jit(solution)/shard_map/ppermute | solution.py:265
  52.8 5.8 %copy-start.3 = (s32[256]{0:T(256)S(1)}, s32[256]{0:T(256)}, u32[]{:S(2)}) copy-start(s32[256]{0:T(256)} %constant.2.clone.table_ref) | copy-start | bytes 3076

commit v3 on v2

--- a/solution.py
+++ b/solution.py
@@ -36,7 +36,14 @@
     (8, 2, 3, 13, 6, 1, 10, 15, 11, 9, 5, 12, 14, 7, 4, 0),
     (0, 5, 4, 7, 2, 13, 11, 14, 3, 10, 8, 6, 1, 9, 15, 12),
 )
-PIECE_AT = np.argsort(np.array(PLACE), axis=1).astype(np.int32)
+PIECE_AT = np.argsort(np.array(PLACE), axis=1)
+PIECE_WORDS = [
+    [
+        int(np.array(sum(int(p) << 4 * i for i, p in enumerate(row[at : at + 8])), np.uint32).astype(np.int32))
+        for row in PIECE_AT
+    ]
+    for at in (0, 8)
+]
 
 
 def split(x):
@@ -75,30 +82,30 @@
         to[...] = source[...]
 
 
-def stack_kernel(counts, *refs):
+def stack_kernel(groups, *refs):
     sources = iter(refs)
-    outs = refs[sum(counts):]
-    for count, out in zip(counts, outs):
-        for slot in range(count):
-            out[slot] = next(sources)[...]
+    for group, out in zip(groups, refs[len(refs) - len(groups) :]):
+        at = 0
+        for count in group:
+            out[at : at + count] = next(sources)[...]
+            at += count
 
 
 def left_kernel(
-    chips, other_ref, same_ref, other_four_ref, four_ref, inv_high, inv_low,
-    high_ref, low_ref, own_ref,
-    panel_high, panel_low, solved,
+    steps, *refs,
 ):
+    count = len(steps)
+    blocks, others, (inv_high, inv_low) = refs[:count], refs[count : 2 * count], refs[2 * count : 2 * count + 2]
+    high_ref, low_ref, own_ref, panel_high, panel_low, solved = refs[2 * count + 2 :]
     column = lax.axis_index("pcol")
     z, core = column // 2, column % 2
-    for slot, step in enumerate(chips):
-        chip = lax.rem(z + CHIPS_Z - step, CHIPS_Z)
-        far = slot == len(chips) - 1
-        pair = (four_ref, other_four_ref) if far else (same_ref, other_ref)
-        for source, where in zip(pair, (core, 1 - core)):
-            rows = chunk(chip * 2 + where)
-            for a in range(2):
-                values = source[a] if far else source[slot, a]
-                panel_high[a, rows, :], panel_low[a, rows, :] = split(values)
+    for which in range(count):
+        for slot, step in enumerate(steps[which]):
+            chip = lax.rem(z + CHIPS_Z - step, CHIPS_Z)
+            for source, where in ((blocks[which], core), (others[which], 1 - core)):
+                rows = chunk(chip * 2 + where)
+                for a in range(2):
+                    panel_high[a, rows, :], panel_low[a, rows, :] = split(source[slot, a])
     for a in range(2):
         high, low = panel_high.at[a], panel_low.at[a]
         solved[:HALF, :] = product(
@@ -107,7 +114,7 @@
         solved[HALF:, :] = product(
             (inv_high[HALF:, :], inv_low[HALF:, :]), (high[...], low[...])
         )
-        own_ref[a] = solved[chunk(column), :]
+        own_ref[0, a] = solved[chunk(column), :]
         high[...], low[...] = split(solved[...].T)
         high_ref[a, :, :HALF], low_ref[a, :, :HALF] = split(
             product((high[...], low[...]), (inv_high[:, :HALF], inv_low[:, :HALF]))
@@ -120,7 +127,7 @@
 
 
 def right_kernel(
-    table_ref, second_ref, third_ref, fourth_ref, left_high, left_low, first_ref, tiles_ref,
+    first_ref, second_ref, third_ref, fourth_ref, left_high, left_low, tiles_ref,
     updated_ref,
     block, panel_high, panel_low, out_sem,
 ):
@@ -129,13 +136,22 @@
     beneath = row >= column
     y, x, core = row // SIDE, row % SIDE, column % 2
 
+    def word(entries):
+        picked = jnp.int32(0)
+        for c, entry in enumerate(entries):
+            picked = jnp.where(column == c, jnp.int32(entry), picked)
+        return picked
+
+    near, far = word(PIECE_WORDS[0]), word(PIECE_WORDS[1])
+
     def place(b):
         for group, source in enumerate((first_ref, second_ref, third_ref, fourth_ref)):
             for slot in range(SIDE):
                 to_y = jnp.where(core == 0, OFFSETS[group], OFFSETS[slot])
                 to_x = jnp.where(core == 0, OFFSETS[slot], OFFSETS[group])
                 at = lax.rem(y + to_y + SIDE, SIDE) * SIDE + lax.rem(x + to_x + SIDE, SIDE)
-                rows = chunk(table_ref[column * GROUPS + at])
+                bits = lax.shift_right_logical(jnp.where(at < 8, near, far), at % 8 * 4)
+                rows = chunk(bits & 15)
                 panel_high[b, rows, :], panel_low[b, rows, :] = split(source[slot, b])
 
     def update(a, b, half):
@@ -194,7 +210,6 @@
 
 VMEM = pl.BlockSpec(memory_space=pltpu.VMEM)
 HBM = pl.BlockSpec(memory_space=pl.ANY)
-SMEM = pl.BlockSpec(memory_space=pltpu.SMEM)
 
 
 def params(mib):
@@ -223,36 +238,37 @@
     return [jax.ShapeDtypeStruct(a.shape, a.dtype) for a in arrays]
 
 
-def meet(pieces, others=()):
+def meet(pieces, others=(), hint=0):
     return pl.pallas_call(
         functools.partial(meet_kernel, len(pieces)),
         out_shape=like(*pieces),
         in_specs=[VMEM] * len(pieces) + [HBM] * len(others),
         out_specs=[VMEM] * len(pieces),
         compiler_params=params(4),
-        cost_estimate=cost(0, 2 * sum(p.size for p in pieces)),
+        cost_estimate=cost(0, hint or 2 * sum(p.size for p in pieces)),
         name="meet",
     )(*pieces, *others)
 
 
-def stacked(*groups):
+def stacked(*groups, others=(), hint=0):
     pieces = [p for group in groups for p in group]
+    sizes = [[p.shape[0] for p in group] for group in groups]
     return pl.pallas_call(
-        functools.partial(stack_kernel, [len(group) for group in groups]),
+        functools.partial(stack_kernel, sizes),
         out_shape=[
-            jax.ShapeDtypeStruct((len(group),) + group[0].shape, jnp.float32)
-            for group in groups
+            jax.ShapeDtypeStruct((sum(size),) + group[0].shape[1:], jnp.float32)
+            for size, group in zip(sizes, groups)
         ],
-        in_specs=[VMEM] * len(pieces),
+        in_specs=[VMEM] * len(pieces) + [HBM] * len(others),
         out_specs=[VMEM] * len(groups),
         compiler_params=params(4),
-        cost_estimate=cost(0, 2 * sum(p.size for p in pieces)),
+        cost_estimate=cost(0, hint or 2 * sum(p.size for p in pieces)),
         name="stack",
-    )(*pieces)
+    )(*pieces, *others)
 
 
 def local(trailing, panel, diag_inverse):
-    piece = panel.transpose(0, 2, 1)
+    piece = panel.transpose(0, 2, 1)[None]
     view = trailing.reshape(2, NB, 2, PARTS, LANES).transpose(0, 1, 3, 2, 4)
     view = view.reshape(2 * NB * STRIDE, LANES)
     whole = jax.ShapeDtypeStruct((NB, NB), jnp.bfloat16)
@@ -274,25 +290,26 @@
         name="load",
     )(view, piece, diag_inverse)
 
-    one, seven = by(1, piece), by(-1, piece)
-    two, six = by(1, one), by(-1, seven)
     turn = [
         (r * GROUPS + c, PLACE[r][c] * GROUPS + r)
         for r in range(GROUPS)
         for c in range(GROUPS)
     ]
     turned = lax.ppermute(piece, ("prow", "pcol"), turn)
-    one, seven, two, six, turned = meet([one, seven, two, six, turned], [tiles])
-
+    one, seven = by(1, piece), by(-1, piece)
+    two, six = by(1, one), by(-1, seven)
+    (turned,) = meet([turned], hint=16777216)
+    (turned,) = meet([turned], [tiles, one, seven])
+    planar = [in_plane(m, turned) for m in ((0, 1), (0, -1), (0, 2))]
+    two, six = meet([two, six], [turned])
     three, five = by(1, two), by(-1, six)
-    planar = [in_plane(m, turned) for m in ((0, 1), (0, -1), (0, 2))]
-    same, first = stacked([kept, one, seven, two, six, three, five], [turned] + planar)
-
-    four = by(1, same[5])
+    (first,) = stacked([turned] + planar, others=[two, six], hint=16777216)
+    (same,) = stacked([kept, one, seven, two, six, three, five], others=[first])
+    four = by(1, same[5:6])
     other, other_four = swap(same), swap(four)
     rest = [in_plane(m, first) for m in ((1, 0), (-1, 0), (2, 0))]
     left_high, left_low, own = pl.pallas_call(
-        functools.partial(left_kernel, (0, 1, 7, 2, 6, 3, 5, 4)),
+        functools.partial(left_kernel, ((0, 1, 7, 2, 6, 3, 5), (4,))),
         out_shape=[pair, pair, *like(piece)],
         in_specs=[VMEM] * 6,
         out_specs=[VMEM] * 3,
@@ -304,12 +321,12 @@
         compiler_params=params(16),
         cost_estimate=cost(20 * NB**3, 6 * NB * NB),
         name="left",
-    )(other, same, other_four, four, inv_high, inv_low)
+    )(same, four, other, other_four, inv_high, inv_low)
 
     updated = pl.pallas_call(
         right_kernel,
         out_shape=jax.ShapeDtypeStruct(view.shape, jnp.float32),
-        in_specs=[SMEM] + [VMEM] * 7,
+        in_specs=[VMEM] * 7,
         out_specs=HBM,
         scratch_shapes=[
             pltpu.VMEM(view.shape, jnp.float32),
@@ -320,9 +337,9 @@
         compiler_params=params(16),
         cost_estimate=cost(18 * NB**3, 12 * NB * NB),
         name="right",
-    )(jnp.asarray(PIECE_AT.reshape(-1)), *rest, left_high, left_low, first, tiles)
+    )(first, *rest, left_high, left_low, tiles)
     updated = updated.reshape(2, NB, PARTS, 2, LANES).transpose(0, 1, 3, 2, 4)
-    return updated.reshape(trailing.shape), own.transpose(0, 2, 1)
+    return updated.reshape(trailing.shape), own[0].transpose(0, 2, 1)
 
 
 def solution(mesh):

time: 62.6 us -> 59.9 us (0.957)
  the two profiles are of different devices: /device:TPU:1 before, /device:TPU:6 now
where the time goes in v3:
time: 59.9 us; the launch traced here: 59.7 us
  starting transfers between devices  23.4 us (39%)
  waiting for transfers between devices  21.6 us (36%)
  Pallas kernels  9.47 us (16%)
  local copies, waits for them, and re-layouts  4.33 us (7%)
  between operations  0.9 us (2%)
    ppermute x7, waiting for transfers between devices, by(): return lax.ppermute(block, 'pcol', along_z(step))  16.1 us
    ppermute x7, starting transfers between devices, by(): return lax.ppermute(block, 'pcol', along_z(step))  13 us
    ppermute x6, starting transfers between devices, in_plane(): return lax.ppermute(piece, ('prow', 'pcol'), pairs)  9.22 us
    pallas_call x1, Pallas kernels, local(): pl.pallas_call(right_kernel, out_shape=jax.ShapeDtypeStruct(view.shape, j...  5.25 us
    unnamed x6, local copies, waits for them, and re-layouts  4.32 us
    pallas_call x1, Pallas kernels, local(): pl.pallas_call(functools.partial(left_kernel, ((0, 1, 7, 2, 6, 3, 5), (4,...  3.26 us
    ppermute x1, waiting for transfers between devices, local(): turned = lax.ppermute(piece, ('prow', 'pcol'), turn)  2.46 us
    ppermute x6, waiting for transfers between devices, in_plane(): return lax.ppermute(piece, ('prow', 'pcol'), pairs)  2.04 us
  transfers between devices with their start and end apart: 16, of which 7 were waited for; matrix products, arithmetic and copies ran while one was open for 0% of the time, Pallas kernels for 7%

profile of v3, /device:TPU:6, one launch (start us, length us, event | category | flops | bytes accessed | tf_op | source)
XLA Modules:
  0.0 59.7 jit_solution(2279246701962059930)
XLA Ops:
  0.6 5.9 %collective-permute-start.2 = (f32[1,2,32,512]{3,2,1,0:T(8,128)}, f32[1,2,32,512]{3,2,1,0:T(8,128)S(1)}, u32[]{:S(2)}, u32[]{:S(2)}) collective-permute-start(f32[1,2,32,512]{3,2,1,0:T(8,128)} %bitcast.17), channel_id=1, source_target_pairs={{0,14},{1,15},{2,0},{3,1},{4,2},{5,3},{6,4},{7,5},{8,6},{9,7},{10,... | collective-permute-start | bytes 393224 | tf_op jit(solution)/shard_map/ppermute | solution.py:278
  6.6 0.0 collective-permute-start.1
  6.6 0.7 %collective-permute-start = (f32[1,2,32,512]{3,2,1,0:T(8,128)}, f32[1,2,32,512]{3,2,1,0:T(8,128)S(1)}, u32[]{:S(2)}, u32[]{:S(2)}) collective-permute-start(f32[1,2,32,512]{3,2,1,0:T(8,128)} %bitcast.19), channel_id=1, source_target_pairs={{0,112},{1,224},{2,96},{3,32},{4,176},{5,144},{6,80},{7,128},{8,19... | collective-permute-start | bytes 393224 | tf_op jit(solution)/shard_map/ppermute | solution.py:298
  7.3 2.4 %collective-permute-done.2.refs_3_.refs_2_ = f32[1,2,32,512]{3,2,1,0:T(8,128)S(1)} collective-permute-done((f32[1,2,32,512]{3,2,1,0:T(8,128)}, f32[1,2,32,512]{3,2,1,0:T(8,128)S(1)}, u32[]{:S(2)}, u32[]{:S(2)}) %collective-permute-start.2) | collective-permute-done | bytes 131104 | tf_op jit(solution)/shard_map/ppermute | solution.py:278
  9.6 3.6 %collective-permute-start.7 = (f32[1,2,32,512]{3,2,1,0:T(8,128)S(1)}, f32[1,2,32,512]{3,2,1,0:T(8,128)S(1)}, u32[]{:S(2)}, u32[]{:S(2)}) collective-permute-start(f32[1,2,32,512]{3,2,1,0:T(8,128)S(1)} %collective-permute-done.2.refs_3_.refs_2_), channel_id=1, source_target_pairs={{0,14},{1,15},{2,0},{3,1},{4,2},{5,3},{6,4},{7,5},{8,6},{9,7},{10,... | collective-permute-start | bytes 393224 | tf_op jit(solution)/shard_map/ppermute | solution.py:278
  13.2 3.6 %collective-permute-done.1.refs_2_.refs_1_ = f32[1,2,32,512]{3,2,1,0:T(8,128)S(1)} collective-permute-done((f32[1,2,32,512]{3,2,1,0:T(8,128)}, f32[1,2,32,512]{3,2,1,0:T(8,128)S(1)}, u32[]{:S(2)}, u32[]{:S(2)}) %collective-permute-start.1) | collective-permute-done | bytes 131104 | tf_op jit(solution)/shard_map/ppermute | solution.py:278
  16.8 0.0 collective-permute-start.6
  16.8 0.0 copy-start
  16.8 2.2 %copy-done = f32[2,512,2,512]{3,2,1,0:T(2,128)S(1)} copy-done((f32[2,512,2,512]{3,2,1,0:T(2,128)S(1)}, f32[2,512,2,512]{3,2,1,0:T(2,128)}, u32[]{:S(2)}) %copy-start) | copy-done | bytes 4194328
  19.0 0.0 copy-start.1
  19.0 1.2 %copy-done.1 = f32[512,512]{1,0:T(8,128)S(1)} copy-done((f32[512,512]{1,0:T(8,128)S(1)}, f32[512,512]{1,0:T(8,128)}, u32[]{:S(2)}) %copy-start.1) | copy-done | bytes 1048600
  20.2 0.0 copy-start.2
  20.2 0.9 %copy-done.2 = f32[2,512,32]{1,2,0:T(8,128)S(1)} copy-done((f32[2,512,32]{1,2,0:T(8,128)S(1)}, f32[2,512,32]{1,2,0:T(8,128)}, u32[]{:S(2)}) %copy-start.2) | copy-done | bytes 131096
  21.1 0.8 %load.1 = (f32[3,512,512]{2,1,0:T(8,128)S(1)}, f32[1,2,32,512]{3,2,1,0:T(8,128)S(1)}, bf16[512,512]{1,0:T(8,128)(2,1)S(1)}, bf16[512,512]{1,0:T(8,128)(2,1)S(1)}) custom-call(f32[8192,128]{1,0:T(8,128)S(1)} %bitcast.16, f32[1,2,32,512]{3,2,1,0:T(8,128)S(1)} %bitcast.20, f32[512,512]{1,0:T(8,128)S(1)} %copy-done.1), custom_call_target="tpu_custom_call" | custom-call | bytes 8388608 | tf_op jit(solution)/shard_map/load/pallas_call | solution.py:283
  21.9 2.5 %collective-permute-done.refs_0_ = f32[1,2,32,512]{3,2,1,0:T(8,128)S(1)} collective-permute-done((f32[1,2,32,512]{3,2,1,0:T(8,128)}, f32[1,2,32,512]{3,2,1,0:T(8,128)S(1)}, u32[]{:S(2)}, u32[]{:S(2)}) %collective-permute-start) | collective-permute-done | bytes 131104 | tf_op jit(solution)/shard_map/ppermute | solution.py:298
  24.4 3.8 %collective-permute-start.5 = (f32[1,2,32,512]{3,2,1,0:T(8,128)S(1)}, f32[1,2,32,512]{3,2,1,0:T(8,128)S(1)}, u32[]{:S(2)}, u32[]{:S(2)}) collective-permute-start(f32[1,2,32,512]{3,2,1,0:T(8,128)S(1)} %meet.4.refs_2_.refs_0_), channel_id=1, source_target_pairs={{0,32},{1,129},{2,34},{3,131},{4,36},{5,133},{6,38},{7,135},{8,40}... | collective-permute-start | bytes 393224 | tf_op jit(solution)/shard_map/ppermute | solution.py:230
  28.2 0.0 collective-permute-start.4
  28.2 3.2 %collective-permute-start.3 = (f32[1,2,32,512]{3,2,1,0:T(8,128)S(1)}, f32[1,2,32,512]{3,2,1,0:T(8,128)S(1)}, u32[]{:S(2)}, u32[]{:S(2)}) collective-permute-start(f32[1,2,32,512]{3,2,1,0:T(8,128)S(1)} %meet.4.refs_2_.refs_0_), channel_id=1, source_target_pairs={{0,16},{1,65},{2,18},{3,67},{4,20},{5,69},{6,22},{7,71},{8,24},{9,... | collective-permute-start | bytes 393224 | tf_op jit(solution)/shard_map/ppermute | solution.py:230
  31.5 0.0 collective-permute-done.7.refs_1_
  31.5 0.0 collective-permute-done.6.refs_0_
  31.5 0.1 collective-permute-start.11
  31.6 3.3 %collective-permute-start.12 = (f32[1,2,32,512]{3,2,1,0:T(8,128)S(1)}, f32[1,2,32,512]{3,2,1,0:T(8,128)S(1)}, u32[]{:S(2)}, u32[]{:S(2)}) collective-permute-start(f32[1,2,32,512]{3,2,1,0:T(8,128)S(1)} %get-tuple-element.13.refs_5_.refs_4_), channel_id=1, source_target_pairs={{0,14},{1,15},{2,0},{3,1},{4,2},{5,3},{6,4},{7,5},{8,6},{9,7},{10,... | collective-permute-start | bytes 393224 | tf_op jit(solution)/shard_map/ppermute | solution.py:278
  34.9 0.0 collective-permute-done.5.refs_3_
  34.9 0.0 collective-permute-done.4.refs_2_
  34.9 0.0 collective-permute-done.3.refs_1_
  35.0 2.8 %collective-permute-done.11.refs_5_ = f32[1,2,32,512]{3,2,1,0:T(8,128)S(1)} collective-permute-done((f32[1,2,32,512]{3,2,1,0:T(8,128)S(1)}, f32[1,2,32,512]{3,2,1,0:T(8,128)S(1)}, u32[]{:S(2)}, u32[]{:S(2)}) %collective-permute-start.11) | collective-permute-done | bytes 131104 | tf_op jit(solution)/shard_map/ppermute | solution.py:278
  37.8 0.0 collective-permute-done.12.refs_6_
  37.8 0.1 stack.3.refs_0_
  37.8 0.1 collective-permute-start.14
  37.9 0.1 collective-permute-start.10
  38.0 0.9 %collective-permute-start.9 = (f32[4,2,32,512]{3,2,1,0:T(8,128)S(1)}, f32[4,2,32,512]{3,2,1,0:T(8,128)S(1)}, u32[]{:S(2)}, u32[]{:S(2)}) collective-permute-start(f32[4,2,32,512]{3,2,1,0:T(8,128)S(1)} %stack.2.refs_7_.first_ref), channel_id=1, source_target_pairs={{0,192},{1,49},{2,194},{3,51},{4,196},{5,53},{6,198},{7,55},{8,200... | collective-permute-start | bytes 1572872 | tf_op jit(solution)/shard_map/ppermute | solution.py:230
  38.9 1.2 %collective-permute-start.8 = (f32[4,2,32,512]{3,2,1,0:T(8,128)S(1)}, f32[4,2,32,512]{3,2,1,0:T(8,128)S(1)}, u32[]{:S(2)}, u32[]{:S(2)}) collective-permute-start(f32[4,2,32,512]{3,2,1,0:T(8,128)S(1)} %stack.2.refs_7_.first_ref), channel_id=1, source_target_pairs={{0,64},{1,17},{2,66},{3,19},{4,68},{5,21},{6,70},{7,23},{8,72},{9,... | collective-permute-start | bytes 1572872 | tf_op jit(solution)/shard_map/ppermute | solution.py:230
  40.1 0.1 collective-permute-start.13
  40.2 7.4 %collective-permute-done.13.refs_1_ = f32[1,2,32,512]{3,2,1,0:T(8,128)S(1)} collective-permute-done((f32[1,2,32,512]{3,2,1,0:T(8,128)S(1)}, f32[1,2,32,512]{3,2,1,0:T(8,128)S(1)}, u32[]{:S(2)}, u32[]{:S(2)}) %collective-permute-start.13) | collective-permute-done | bytes 131104 | tf_op jit(solution)/shard_map/ppermute | solution.py:278
  47.6 0.4 collective-permute-start.15
  48.0 1.0 %collective-permute-done.15.refs_3_ = f32[1,2,32,512]{3,2,1,0:T(8,128)S(1)} collective-permute-done((f32[1,2,32,512]{3,2,1,0:T(8,128)S(1)}, f32[1,2,32,512]{3,2,1,0:T(8,128)S(1)}, u32[]{:S(2)}, u32[]{:S(2)}) %collective-permute-start.15) | collective-permute-done | bytes 131104 | tf_op jit(solution)/shard_map/ppermute | solution.py:281
  49.0 0.0 collective-permute-done.14.refs_2_
  49.0 3.3 %left.1 = (bf16[2,512,512]{2,1,0:T(8,128)(2,1)S(1)}, bf16[2,512,512]{2,1,0:T(8,128)(2,1)S(1)}, f32[1,2,32,512]{3,2,1,0:T(8,128)}) custom-call(f32[7,2,32,512]{3,2,1,0:T(8,128)S(1)} %stack.3.refs_0_, f32[1,2,32,512]{3,2,1,0:T(8,128)S(1)} %collective-permute-done.13.refs_1_, f32[7,2,32,512]{3,2,1,0:T(8,128)S(1)} %collective-permute-done.14.refs_2_, ...), custom_call_target="tpu_custom_call" | custom-call | flops 2684354560 | bytes 6291456 | tf_op jit(solution)/shard_map/left/pallas_call | solution.py:311
  52.3 0.0 collective-permute-done.10.fourth_ref
  52.3 0.0 collective-permute-done.9.third_ref
  52.3 2.0 %collective-permute-done.8.second_ref = f32[4,2,32,512]{3,2,1,0:T(8,128)S(1)} collective-permute-done((f32[4,2,32,512]{3,2,1,0:T(8,128)S(1)}, f32[4,2,32,512]{3,2,1,0:T(8,128)S(1)}, u32[]{:S(2)}, u32[]{:S(2)}) %collective-permute-start.8) | collective-permute-done | bytes 524320 | tf_op jit(solution)/shard_map/ppermute | solution.py:230
  54.3 5.3 %right.1 = f32[8192,128]{1,0:T(8,128)} custom-call(f32[4,2,32,512]{3,2,1,0:T(8,128)S(1)} %stack.2.refs_7_.first_ref, f32[4,2,32,512]{3,2,1,0:T(8,128)S(1)} %collective-permute-done.8.second_ref, f32[4,2,32,512]{3,2,1,0:T(8,128)S(1)} %collective-permute-done.9.third_ref, f32[4,2,32,512]{3,2,1,0:T(8,128)S(1)} %collective-permute-done.10.fourth_ref, ...), custom_call_target="tpu_custom_call" | custom-call | flops 2415919104 | bytes 12582912 | tf_op jit(solution)/shard_map/right/pallas_call | solution.py:326
  (5 shorter events, 0.1 us)
Async XLA Ops:
  0.6 9.0 %collective-permute-start.2 = (f32[1,2,32,512]{3,2,1,0:T(8,128)}, f32[1,2,32,512]{3,2,1,0:T(8,128)S(1)}, u32[]{:S(2)}, u32[]{:S(2)}) collective-permute-start(f32[1,2,32,512]{3,2,1,0:T(8,128)} %bitcast.17), channel_id=1, source_target_pairs={{0,14},{1,15},{2,0},{3,1},{4,2},{5,3},{6,4},{7,5},{8,6},{9,7},{10,... | collective-permute-start | bytes 393224 | tf_op jit(solution)/shard_map/ppermute | solution.py:278
  6.6 10.2 %collective-permute-start.1 = (f32[1,2,32,512]{3,2,1,0:T(8,128)}, f32[1,2,32,512]{3,2,1,0:T(8,128)S(1)}, u32[]{:S(2)}, u32[]{:S(2)}) collective-permute-start(f32[1,2,32,512]{3,2,1,0:T(8,128)} %bitcast.18), channel_id=1, source_target_pairs={{0,2},{1,3},{2,4},{3,5},{4,6},{5,7},{6,8},{7,9},{8,10},{9,11},{10,... | collective-permute-start | bytes 393224 | tf_op jit(solution)/shard_map/ppermute | solution.py:278
  6.6 17.8 %collective-permute-start = (f32[1,2,32,512]{3,2,1,0:T(8,128)}, f32[1,2,32,512]{3,2,1,0:T(8,128)S(1)}, u32[]{:S(2)}, u32[]{:S(2)}) collective-permute-start(f32[1,2,32,512]{3,2,1,0:T(8,128)} %bitcast.19), channel_id=1, source_target_pairs={{0,112},{1,224},{2,96},{3,32},{4,176},{5,144},{6,80},{7,128},{8,19... | collective-permute-start | bytes 393224 | tf_op jit(solution)/shard_map/ppermute | solution.py:298
  9.6 21.8 %collective-permute-start.7 = (f32[1,2,32,512]{3,2,1,0:T(8,128)S(1)}, f32[1,2,32,512]{3,2,1,0:T(8,128)S(1)}, u32[]{:S(2)}, u32[]{:S(2)}) collective-permute-start(f32[1,2,32,512]{3,2,1,0:T(8,128)S(1)} %collective-permute-done.2.refs_3_.refs_2_), channel_id=1, source_target_pairs={{0,14},{1,15},{2,0},{3,1},{4,2},{5,3},{6,4},{7,5},{8,6},{9,7},{10,... | collective-permute-start | bytes 393224 | tf_op jit(solution)/shard_map/ppermute | solution.py:278
  16.8 14.7 %collective-permute-start.6 = (f32[1,2,32,512]{3,2,1,0:T(8,128)S(1)}, f32[1,2,32,512]{3,2,1,0:T(8,128)S(1)}, u32[]{:S(2)}, u32[]{:S(2)}) collective-permute-start(f32[1,2,32,512]{3,2,1,0:T(8,128)S(1)} %collective-permute-done.1.refs_2_.refs_1_), channel_id=1, source_target_pairs={{0,2},{1,3},{2,4},{3,5},{4,6},{5,7},{6,8},{7,9},{8,10},{9,11},{10,... | collective-permute-start | bytes 393224 | tf_op jit(solution)/shard_map/ppermute | solution.py:278
  16.8 2.2 %copy-start = (f32[2,512,2,512]{3,2,1,0:T(2,128)S(1)}, f32[2,512,2,512]{3,2,1,0:T(2,128)}, u32[]{:S(2)}) copy-start(f32[2,512,2,512]{3,2,1,0:T(2,128)} %param.3) | copy-start | bytes 12582916
  19.0 1.2 %copy-start.1 = (f32[512,512]{1,0:T(8,128)S(1)}, f32[512,512]{1,0:T(8,128)}, u32[]{:S(2)}) copy-start(f32[512,512]{1,0:T(8,128)} %inverse_ref.1) | copy-start | bytes 3145732
  20.2 0.9 %copy-start.2 = (f32[2,512,32]{1,2,0:T(8,128)S(1)}, f32[2,512,32]{1,2,0:T(8,128)}, u32[]{:S(2)}) copy-start(f32[2,512,32]{1,2,0:T(8,128)} %param.4) | copy-start | bytes 393220
  24.4 10.5 %collective-permute-start.5 = (f32[1,2,32,512]{3,2,1,0:T(8,128)S(1)}, f32[1,2,32,512]{3,2,1,0:T(8,128)S(1)}, u32[]{:S(2)}, u32[]{:S(2)}) collective-permute-start(f32[1,2,32,512]{3,2,1,0:T(8,128)S(1)} %meet.4.refs_2_.refs_0_), channel_id=1, source_target_pairs={{0,32},{1,129},{2,34},{3,131},{4,36},{5,133},{6,38},{7,135},{8,40}... | collective-permute-start | bytes 393224 | tf_op jit(solution)/shard_map/ppermute | solution.py:230
  28.2 6.7 %collective-permute-start.4 = (f32[1,2,32,512]{3,2,1,0:T(8,128)S(1)}, f32[1,2,32,512]{3,2,1,0:T(8,128)S(1)}, u32[]{:S(2)}, u32[]{:S(2)}) collective-permute-start(f32[1,2,32,512]{3,2,1,0:T(8,128)S(1)} %meet.4.refs_2_.refs_0_), channel_id=1, source_target_pairs={{0,48},{1,193},{2,50},{3,195},{4,52},{5,197},{6,54},{7,199},{8,56}... | collective-permute-start | bytes 393224 | tf_op jit(solution)/shard_map/ppermute | solution.py:230
  28.2 6.7 %collective-permute-start.3 = (f32[1,2,32,512]{3,2,1,0:T(8,128)S(1)}, f32[1,2,32,512]{3,2,1,0:T(8,128)S(1)}, u32[]{:S(2)}, u32[]{:S(2)}) collective-permute-start(f32[1,2,32,512]{3,2,1,0:T(8,128)S(1)} %meet.4.refs_2_.refs_0_), channel_id=1, source_target_pairs={{0,16},{1,65},{2,18},{3,67},{4,20},{5,69},{6,22},{7,71},{8,24},{9,... | collective-permute-start | bytes 393224 | tf_op jit(solution)/shard_map/ppermute | solution.py:230
  31.5 6.3 %collective-permute-start.11 = (f32[1,2,32,512]{3,2,1,0:T(8,128)S(1)}, f32[1,2,32,512]{3,2,1,0:T(8,128)S(1)}, u32[]{:S(2)}, u32[]{:S(2)}) collective-permute-start(f32[1,2,32,512]{3,2,1,0:T(8,128)S(1)} %get-tuple-element.12.refs_4_.refs_3_), channel_id=1, source_target_pairs={{0,2},{1,3},{2,4},{3,5},{4,6},{5,7},{6,8},{7,9},{8,10},{9,11},{10,... | collective-permute-start | bytes 393224 | tf_op jit(solution)/shard_map/ppermute | solution.py:278
  31.6 6.2 %collective-permute-start.12 = (f32[1,2,32,512]{3,2,1,0:T(8,128)S(1)}, f32[1,2,32,512]{3,2,1,0:T(8,128)S(1)}, u32[]{:S(2)}, u32[]{:S(2)}) collective-permute-start(f32[1,2,32,512]{3,2,1,0:T(8,128)S(1)} %get-tuple-element.13.refs_5_.refs_4_), channel_id=1, source_target_pairs={{0,14},{1,15},{2,0},{3,1},{4,2},{5,3},{6,4},{7,5},{8,6},{9,7},{10,... | collective-permute-start | bytes 393224 | tf_op jit(solution)/shard_map/ppermute | solution.py:278
  37.8 11.2 %collective-permute-start.14 = (f32[7,2,32,512]{3,2,1,0:T(8,128)S(1)}, f32[7,2,32,512]{3,2,1,0:T(8,128)S(1)}, u32[]{:S(2)}, u32[]{:S(2)}) collective-permute-start(f32[7,2,32,512]{3,2,1,0:T(8,128)S(1)} %stack.3.refs_0_), channel_id=1, source_target_pairs={{0,1},{1,0},{2,3},{3,2},{4,5},{5,4},{6,7},{7,6},{8,9},{9,8},{10,11... | collective-permute-start | bytes 2752520 | tf_op jit(solution)/shard_map/ppermute | solution.py:281
  37.9 14.3 %collective-permute-start.10 = (f32[4,2,32,512]{3,2,1,0:T(8,128)S(1)}, f32[4,2,32,512]{3,2,1,0:T(8,128)S(1)}, u32[]{:S(2)}, u32[]{:S(2)}) collective-permute-start(f32[4,2,32,512]{3,2,1,0:T(8,128)S(1)} %stack.2.refs_7_.first_ref), channel_id=1, source_target_pairs={{0,128},{1,33},{2,130},{3,35},{4,132},{5,37},{6,134},{7,39},{8,136... | collective-permute-start | bytes 1572872 | tf_op jit(solution)/shard_map/ppermute | solution.py:230
  38.0 14.3 %collective-permute-start.9 = (f32[4,2,32,512]{3,2,1,0:T(8,128)S(1)}, f32[4,2,32,512]{3,2,1,0:T(8,128)S(1)}, u32[]{:S(2)}, u32[]{:S(2)}) collective-permute-start(f32[4,2,32,512]{3,2,1,0:T(8,128)S(1)} %stack.2.refs_7_.first_ref), channel_id=1, source_target_pairs={{0,192},{1,49},{2,194},{3,51},{4,196},{5,53},{6,198},{7,55},{8,200... | collective-permute-start | bytes 1572872 | tf_op jit(solution)/shard_map/ppermute | solution.py:230
  38.9 15.4 %collective-permute-start.8 = (f32[4,2,32,512]{3,2,1,0:T(8,128)S(1)}, f32[4,2,32,512]{3,2,1,0:T(8,128)S(1)}, u32[]{:S(2)}, u32[]{:S(2)}) collective-permute-start(f32[4,2,32,512]{3,2,1,0:T(8,128)S(1)} %stack.2.refs_7_.first_ref), channel_id=1, source_target_pairs={{0,64},{1,17},{2,66},{3,19},{4,68},{5,21},{6,70},{7,23},{8,72},{9,... | collective-permute-start | bytes 1572872 | tf_op jit(solution)/shard_map/ppermute | solution.py:230
  40.1 7.5 %collective-permute-start.13 = (f32[1,2,32,512]{3,2,1,0:T(8,128)S(1)}, f32[1,2,32,512]{3,2,1,0:T(8,128)S(1)}, u32[]{:S(2)}, u32[]{:S(2)}) collective-permute-start(f32[1,2,32,512]{3,2,1,0:T(8,128)S(1)} %slice.4), channel_id=1, source_target_pairs={{0,2},{1,3},{2,4},{3,5},{4,6},{5,7},{6,8},{7,9},{8,10},{9,11},{10,... | collective-permute-start | bytes 393224 | tf_op jit(solution)/shard_map/ppermute | solution.py:278
  47.6 1.4 %collective-permute-start.15 = (f32[1,2,32,512]{3,2,1,0:T(8,128)S(1)}, f32[1,2,32,512]{3,2,1,0:T(8,128)S(1)}, u32[]{:S(2)}, u32[]{:S(2)}) collective-permute-start(f32[1,2,32,512]{3,2,1,0:T(8,128)S(1)} %collective-permute-done.13.refs_1_), channel_id=1, source_target_pairs={{0,1},{1,0},{2,3},{3,2},{4,5},{5,4},{6,7},{7,6},{8,9},{9,8},{10,11... | collective-permute-start | bytes 393224 | tf_op jit(solution)/shard_map/ppermute | solution.py:281

commit v4 on v3

--- a/solution.py
+++ b/solution.py
@@ -67,13 +67,34 @@
     return pl.ds((a * NB + start) * STRIDE + j * 2 + b, count, stride=STRIDE)
 
 
-def load_kernel(view_ref, piece_ref, inverse_ref, tiles_ref, kept_ref, high_ref, low_ref):
-    kept_ref[...] = piece_ref[...]
-    high_ref[...], low_ref[...] = split(inverse_ref[...])
+def prepare_kernel(piece_ref, inverse_ref, kept_ref, high_ref, low_ref, inverse, sems):
+    fetches = [
+        pltpu.make_async_copy(inverse_ref, inverse, sems.at[0]),
+        pltpu.make_async_copy(piece_ref, kept_ref, sems.at[1]),
+    ]
+    for fetch in fetches:
+        fetch.start()
+    fetches[0].wait()
+    high_ref[...], low_ref[...] = split(inverse[...])
+    fetches[1].wait()
+
+
+def load_kernel(view_ref, tiles_ref, block, sems):
+    fetches = [
+        pltpu.make_async_copy(
+            view_ref.at[pl.ds(a * NB * STRIDE, NB * STRIDE)],
+            block.at[pl.ds(a * NB * STRIDE, NB * STRIDE)],
+            sems.at[a],
+        )
+        for a in range(2)
+    ]
+    for fetch in fetches:
+        fetch.start()
     for a in range(2):
+        fetches[a].wait()
         for b in range(a + 1):
             for j in range(PARTS):
-                tiles_ref[a + b, :, j * LANES : (j + 1) * LANES] = view_ref[lines(a, b, j), :]
+                tiles_ref[a + b, :, j * LANES : (j + 1) * LANES] = block[lines(a, b, j), :]
 
 
 def meet_kernel(count, *refs):
@@ -280,15 +301,26 @@
     def swap(block):
         return lax.ppermute(block, "pcol", [(i, i ^ 1) for i in range(GROUPS)])
 
-    tiles, kept, inv_high, inv_low = pl.pallas_call(
+    kept, inv_high, inv_low = pl.pallas_call(
+        prepare_kernel,
+        out_shape=[*like(piece), whole, whole],
+        in_specs=[pl.BlockSpec(memory_space=pltpu.HBM)] * 2,
+        out_specs=[VMEM] * 3,
+        scratch_shapes=[pltpu.VMEM((NB, NB), jnp.float32), pltpu.SemaphoreType.DMA((2,))],
+        compiler_params=params(8),
+        cost_estimate=cost(0, 2 * NB * NB),
+        name="prepare",
+    )(piece, diag_inverse)
+    (tiles,) = pl.pallas_call(
         load_kernel,
-        out_shape=[jax.ShapeDtypeStruct((3, NB, NB), jnp.float32), *like(piece), whole, whole],
-        in_specs=[VMEM] * 3,
-        out_specs=[VMEM] * 4,
+        out_shape=[jax.ShapeDtypeStruct((3, NB, NB), jnp.float32)],
+        in_specs=[HBM],
+        out_specs=[VMEM],
+        scratch_shapes=[pltpu.VMEM(view.shape, jnp.float32), pltpu.SemaphoreType.DMA((2,))],
         compiler_params=params(12),
         cost_estimate=cost(0, 8 * NB * NB),
         name="load",
-    )(view, piece, diag_inverse)
+    )(view)
 
     turn = [
         (r * GROUPS + c, PLACE[r][c] * GROUPS + r)
@@ -299,7 +331,7 @@
     one, seven = by(1, piece), by(-1, piece)
     two, six = by(1, one), by(-1, seven)
     (turned,) = meet([turned], hint=16777216)
-    (turned,) = meet([turned], [tiles, one, seven])
+    (turned,) = meet([turned], [inv_high, one, seven])
     planar = [in_plane(m, turned) for m in ((0, 1), (0, -1), (0, 2))]
     two, six = meet([two, six], [turned])
     three, five = by(1, two), by(-1, six)

time: 59.9 us -> 58.4 us (0.975)
  local copies, waits for them, and re-layouts: 4.33 us -> 2.14 us
  starting transfers between devices: 23.4 us -> 22.5 us
  Pallas kernels: 9.47 us -> 10.1 us
    ppermute x1, waiting for transfers between devices: 2.46 us -> 5.08 us  [local(): turned = lax.ppermute(piece, ('prow', 'pcol'), turn)]
    unnamed x6, local copies, waits for them, and re-layouts: 4.32 us -> 2.13 us
    ppermute x6, waiting for transfers between devices: 2.04 us -> 0.44 us  [in_plane(): return lax.ppermute(piece, ('prow', 'pcol'), pairs)]
    ppermute x2, waiting for transfers between devices: 0.99 us -> 0.01 us  [swap(): return lax.ppermute(block, 'pcol', [(i, i ^ 1) for i in range(GROUPS)])]
    ppermute x6, starting transfers between devices: 9.22 us -> 8.36 us  [in_plane(): return lax.ppermute(piece, ('prow', 'pcol'), pairs)]
  transfers between devices with their start and end apart: 16 -> 16, of which waited for: 7 -> 7; matrix products, arithmetic and copies ran while one was open for 0% -> 0% of each run, Pallas kernels for 7% -> 8%
where the time goes in v4:
time: 58.4 us; the launch traced here: 57.7 us
  starting transfers between devices  22.5 us (39%)
  waiting for transfers between devices  22 us (38%)
  Pallas kernels  10.1 us (17%)
  local copies, waits for them, and re-layouts  2.14 us (4%)
  between operations  0.92 us (2%)
    ppermute x7, waiting for transfers between devices, by(): return lax.ppermute(block, 'pcol', along_z(step))  16.5 us
    ppermute x7, starting transfers between devices, by(): return lax.ppermute(block, 'pcol', along_z(step))  13 us
    ppermute x6, starting transfers between devices, in_plane(): return lax.ppermute(piece, ('prow', 'pcol'), pairs)  8.36 us
    pallas_call x1, Pallas kernels, local(): pl.pallas_call(right_kernel, out_shape=jax.ShapeDtypeStruct(view.shape, j...  5.25 us
    ppermute x1, waiting for transfers between devices, local(): turned = lax.ppermute(piece, ('prow', 'pcol'), turn)  5.08 us
    pallas_call x1, Pallas kernels, local(): pl.pallas_call(functools.partial(left_kernel, ((0, 1, 7, 2, 6, 3, 5), (4,...  3.27 us
    unnamed x6, local copies, waits for them, and re-layouts  2.13 us
  transfers between devices with their start and end apart: 16, of which 7 were waited for; matrix products, arithmetic and copies ran while one was open for 0% of the time, Pallas kernels for 8%

profile of v4, /device:TPU:6, one launch (start us, length us, event | category | flops | bytes accessed | tf_op | source)
XLA Modules:
  0.0 57.7 jit_solution(1940744831355610847)
XLA Ops:
  0.6 0.0 copy-start
  0.6 5.9 %collective-permute-start.2 = (f32[1,2,32,512]{3,2,1,0:T(8,128)}, f32[1,2,32,512]{3,2,1,0:T(8,128)S(1)}, u32[]{:S(2)}, u32[]{:S(2)}) collective-permute-start(f32[1,2,32,512]{3,2,1,0:T(8,128)} %bitcast.17), channel_id=1, source_target_pairs={{0,14},{1,15},{2,0},{3,1},{4,2},{5,3},{6,4},{7,5},{8,6},{9,7},{10,... | collective-permute-start | bytes 393224 | tf_op jit(solution)/shard_map/ppermute | solution.py:299
  6.6 0.0 collective-permute-start.1
  6.6 0.7 %collective-permute-start = (f32[1,2,32,512]{3,2,1,0:T(8,128)}, f32[1,2,32,512]{3,2,1,0:T(8,128)S(1)}, u32[]{:S(2)}, u32[]{:S(2)}) collective-permute-start(f32[1,2,32,512]{3,2,1,0:T(8,128)} %bitcast.19), channel_id=1, source_target_pairs={{0,112},{1,224},{2,96},{3,32},{4,176},{5,144},{6,80},{7,128},{8,19... | collective-permute-start | bytes 393224 | tf_op jit(solution)/shard_map/ppermute | solution.py:330
  7.3 2.4 %collective-permute-done.2.refs_3_.refs_2_ = f32[1,2,32,512]{3,2,1,0:T(8,128)S(1)} collective-permute-done((f32[1,2,32,512]{3,2,1,0:T(8,128)}, f32[1,2,32,512]{3,2,1,0:T(8,128)S(1)}, u32[]{:S(2)}, u32[]{:S(2)}) %collective-permute-start.2) | collective-permute-done | bytes 131104 | tf_op jit(solution)/shard_map/ppermute | solution.py:299
  9.6 3.6 %collective-permute-start.7 = (f32[1,2,32,512]{3,2,1,0:T(8,128)S(1)}, f32[1,2,32,512]{3,2,1,0:T(8,128)S(1)}, u32[]{:S(2)}, u32[]{:S(2)}) collective-permute-start(f32[1,2,32,512]{3,2,1,0:T(8,128)S(1)} %collective-permute-done.2.refs_3_.refs_2_), channel_id=1, source_target_pairs={{0,14},{1,15},{2,0},{3,1},{4,2},{5,3},{6,4},{7,5},{8,6},{9,7},{10,... | collective-permute-start | bytes 393224 | tf_op jit(solution)/shard_map/ppermute | solution.py:299
  13.2 3.6 %collective-permute-done.1.refs_2_.refs_1_ = f32[1,2,32,512]{3,2,1,0:T(8,128)S(1)} collective-permute-done((f32[1,2,32,512]{3,2,1,0:T(8,128)}, f32[1,2,32,512]{3,2,1,0:T(8,128)S(1)}, u32[]{:S(2)}, u32[]{:S(2)}) %collective-permute-start.1) | collective-permute-done | bytes 131104 | tf_op jit(solution)/shard_map/ppermute | solution.py:299
  16.8 0.0 collective-permute-start.6
  16.8 0.0 copy-start.1
  16.8 1.2 %copy-done.1 = f32[512,512]{1,0:T(8,128)S(1)} copy-done((f32[512,512]{1,0:T(8,128)S(1)}, f32[512,512]{1,0:T(8,128)}, u32[]{:S(2)}) %copy-start.1) | copy-done | bytes 1048600
  18.0 0.0 copy-start.2
  18.0 0.9 %copy-done.2 = f32[2,512,32]{1,2,0:T(8,128)S(1)} copy-done((f32[2,512,32]{1,2,0:T(8,128)S(1)}, f32[2,512,32]{1,2,0:T(8,128)}, u32[]{:S(2)}) %copy-start.2) | copy-done | bytes 131096
  18.9 0.4 prepare.1
  19.3 5.1 %collective-permute-done.refs_0_ = f32[1,2,32,512]{3,2,1,0:T(8,128)S(1)} collective-permute-done((f32[1,2,32,512]{3,2,1,0:T(8,128)}, f32[1,2,32,512]{3,2,1,0:T(8,128)S(1)}, u32[]{:S(2)}, u32[]{:S(2)}) %collective-permute-start) | collective-permute-done | bytes 131104 | tf_op jit(solution)/shard_map/ppermute | solution.py:330
  24.5 1.2 %collective-permute-start.5 = (f32[1,2,32,512]{3,2,1,0:T(8,128)S(1)}, f32[1,2,32,512]{3,2,1,0:T(8,128)S(1)}, u32[]{:S(2)}, u32[]{:S(2)}) collective-permute-start(f32[1,2,32,512]{3,2,1,0:T(8,128)S(1)} %meet.4.refs_2_.refs_0_), channel_id=1, source_target_pairs={{0,32},{1,129},{2,34},{3,131},{4,36},{5,133},{6,38},{7,135},{8,40}... | collective-permute-start | bytes 393224 | tf_op jit(solution)/shard_map/ppermute | solution.py:251
  25.6 0.0 collective-permute-start.4
  25.6 3.2 %collective-permute-start.3 = (f32[1,2,32,512]{3,2,1,0:T(8,128)S(1)}, f32[1,2,32,512]{3,2,1,0:T(8,128)S(1)}, u32[]{:S(2)}, u32[]{:S(2)}) collective-permute-start(f32[1,2,32,512]{3,2,1,0:T(8,128)S(1)} %meet.4.refs_2_.refs_0_), channel_id=1, source_target_pairs={{0,16},{1,65},{2,18},{3,67},{4,20},{5,69},{6,22},{7,71},{8,24},{9,... | collective-permute-start | bytes 393224 | tf_op jit(solution)/shard_map/ppermute | solution.py:251
  28.9 0.0 collective-permute-done.7.refs_1_
  28.9 0.0 collective-permute-done.6.refs_0_
  28.9 0.1 collective-permute-start.11
  29.0 3.3 %collective-permute-start.12 = (f32[1,2,32,512]{3,2,1,0:T(8,128)S(1)}, f32[1,2,32,512]{3,2,1,0:T(8,128)S(1)}, u32[]{:S(2)}, u32[]{:S(2)}) collective-permute-start(f32[1,2,32,512]{3,2,1,0:T(8,128)S(1)} %get-tuple-element.12.refs_5_.refs_4_), channel_id=1, source_target_pairs={{0,14},{1,15},{2,0},{3,1},{4,2},{5,3},{6,4},{7,5},{8,6},{9,7},{10,... | collective-permute-start | bytes 393224 | tf_op jit(solution)/shard_map/ppermute | solution.py:299
  32.3 0.0 collective-permute-done.5.refs_3_
  32.3 0.1 collective-permute-done.4.refs_2_
  32.4 0.0 collective-permute-done.3.refs_1_
  32.5 3.2 %collective-permute-done.11.refs_5_ = f32[1,2,32,512]{3,2,1,0:T(8,128)S(1)} collective-permute-done((f32[1,2,32,512]{3,2,1,0:T(8,128)S(1)}, f32[1,2,32,512]{3,2,1,0:T(8,128)S(1)}, u32[]{:S(2)}, u32[]{:S(2)}) %collective-permute-start.11) | collective-permute-done | bytes 131104 | tf_op jit(solution)/shard_map/ppermute | solution.py:299
  35.7 0.0 collective-permute-done.12.refs_6_
  35.7 0.1 stack.3.refs_0_
  35.8 0.1 collective-permute-start.14
  35.9 1.9 %collective-permute-start.10 = (f32[4,2,32,512]{3,2,1,0:T(8,128)S(1)}, f32[4,2,32,512]{3,2,1,0:T(8,128)S(1)}, u32[]{:S(2)}, u32[]{:S(2)}) collective-permute-start(f32[4,2,32,512]{3,2,1,0:T(8,128)S(1)} %stack.2.refs_7_.first_ref), channel_id=1, source_target_pairs={{0,128},{1,33},{2,130},{3,35},{4,132},{5,37},{6,134},{7,39},{8,136... | collective-permute-start | bytes 1572872 | tf_op jit(solution)/shard_map/ppermute | solution.py:251
  37.8 0.0 collective-permute-start.9
  37.8 2.0 %collective-permute-start.8 = (f32[4,2,32,512]{3,2,1,0:T(8,128)S(1)}, f32[4,2,32,512]{3,2,1,0:T(8,128)S(1)}, u32[]{:S(2)}, u32[]{:S(2)}) collective-permute-start(f32[4,2,32,512]{3,2,1,0:T(8,128)S(1)} %stack.2.refs_7_.first_ref), channel_id=1, source_target_pairs={{0,64},{1,17},{2,66},{3,19},{4,68},{5,21},{6,70},{7,23},{8,72},{9,... | collective-permute-start | bytes 1572872 | tf_op jit(solution)/shard_map/ppermute | solution.py:251
  39.8 0.1 collective-permute-start.13
  39.9 7.3 %collective-permute-done.13.refs_1_ = f32[1,2,32,512]{3,2,1,0:T(8,128)S(1)} collective-permute-done((f32[1,2,32,512]{3,2,1,0:T(8,128)S(1)}, f32[1,2,32,512]{3,2,1,0:T(8,128)S(1)}, u32[]{:S(2)}, u32[]{:S(2)}) %collective-permute-start.13) | collective-permute-done | bytes 131104 | tf_op jit(solution)/shard_map/ppermute | solution.py:299
  47.2 0.4 collective-permute-start.15
  47.6 0.0 copy-done
  47.6 1.0 %load.1.tiles_ref = f32[3,512,512]{2,1,0:T(8,128)S(1)} custom-call(f32[8192,128]{1,0:T(8,128)S(1)} %bitcast.16), custom_call_target="tpu_custom_call" | custom-call | bytes 8388608 | tf_op jit(solution)/shard_map/load/pallas_call | solution.py:314
  48.6 0.0 collective-permute-done.15.refs_3_
  48.6 0.0 collective-permute-done.14.refs_2_
  48.6 3.3 %left.1 = (bf16[2,512,512]{2,1,0:T(8,128)(2,1)S(1)}, bf16[2,512,512]{2,1,0:T(8,128)(2,1)S(1)}, f32[1,2,32,512]{3,2,1,0:T(8,128)}) custom-call(f32[7,2,32,512]{3,2,1,0:T(8,128)S(1)} %stack.3.refs_0_, f32[1,2,32,512]{3,2,1,0:T(8,128)S(1)} %collective-permute-done.13.refs_1_, f32[7,2,32,512]{3,2,1,0:T(8,128)S(1)} %collective-permute-done.14.refs_2_, ...), custom_call_target="tpu_custom_call" | custom-call | flops 2684354560 | bytes 6291456 | tf_op jit(solution)/shard_map/left/pallas_call | solution.py:343
  51.9 0.0 collective-permute-done.10.fourth_ref
  51.9 0.0 collective-permute-done.9.third_ref
  51.9 0.3 collective-permute-done.8.second_ref
  52.2 5.3 %right.1 = f32[8192,128]{1,0:T(8,128)} custom-call(f32[4,2,32,512]{3,2,1,0:T(8,128)S(1)} %stack.2.refs_7_.first_ref, f32[4,2,32,512]{3,2,1,0:T(8,128)S(1)} %collective-permute-done.8.second_ref, f32[4,2,32,512]{3,2,1,0:T(8,128)S(1)} %collective-permute-done.9.third_ref, f32[4,2,32,512]{3,2,1,0:T(8,128)S(1)} %collective-permute-done.10.fourth_ref, ...), custom_call_target="tpu_custom_call" | custom-call | flops 2415919104 | bytes 12582912 | tf_op jit(solution)/shard_map/right/pallas_call | solution.py:358
  (5 shorter events, 0.1 us)
Async XLA Ops:
  0.6 47.0 %copy-start = (f32[2,512,2,512]{3,2,1,0:T(2,128)S(1)}, f32[2,512,2,512]{3,2,1,0:T(2,128)}, u32[]{:S(2)}) copy-start(f32[2,512,2,512]{3,2,1,0:T(2,128)} %param.3) | copy-start | bytes 12582916
  0.6 9.0 %collective-permute-start.2 = (f32[1,2,32,512]{3,2,1,0:T(8,128)}, f32[1,2,32,512]{3,2,1,0:T(8,128)S(1)}, u32[]{:S(2)}, u32[]{:S(2)}) collective-permute-start(f32[1,2,32,512]{3,2,1,0:T(8,128)} %bitcast.17), channel_id=1, source_target_pairs={{0,14},{1,15},{2,0},{3,1},{4,2},{5,3},{6,4},{7,5},{8,6},{9,7},{10,... | collective-permute-start | bytes 393224 | tf_op jit(solution)/shard_map/ppermute | solution.py:299
  6.6 10.2 %collective-permute-start.1 = (f32[1,2,32,512]{3,2,1,0:T(8,128)}, f32[1,2,32,512]{3,2,1,0:T(8,128)S(1)}, u32[]{:S(2)}, u32[]{:S(2)}) collective-permute-start(f32[1,2,32,512]{3,2,1,0:T(8,128)} %bitcast.18), channel_id=1, source_target_pairs={{0,2},{1,3},{2,4},{3,5},{4,6},{5,7},{6,8},{7,9},{8,10},{9,11},{10,... | collective-permute-start | bytes 393224 | tf_op jit(solution)/shard_map/ppermute | solution.py:299
  6.6 17.8 %collective-permute-start = (f32[1,2,32,512]{3,2,1,0:T(8,128)}, f32[1,2,32,512]{3,2,1,0:T(8,128)S(1)}, u32[]{:S(2)}, u32[]{:S(2)}) collective-permute-start(f32[1,2,32,512]{3,2,1,0:T(8,128)} %bitcast.19), channel_id=1, source_target_pairs={{0,112},{1,224},{2,96},{3,32},{4,176},{5,144},{6,80},{7,128},{8,19... | collective-permute-start | bytes 393224 | tf_op jit(solution)/shard_map/ppermute | solution.py:330
  9.6 19.2 %collective-permute-start.7 = (f32[1,2,32,512]{3,2,1,0:T(8,128)S(1)}, f32[1,2,32,512]{3,2,1,0:T(8,128)S(1)}, u32[]{:S(2)}, u32[]{:S(2)}) collective-permute-start(f32[1,2,32,512]{3,2,1,0:T(8,128)S(1)} %collective-permute-done.2.refs_3_.refs_2_), channel_id=1, source_target_pairs={{0,14},{1,15},{2,0},{3,1},{4,2},{5,3},{6,4},{7,5},{8,6},{9,7},{10,... | collective-permute-start | bytes 393224 | tf_op jit(solution)/shard_map/ppermute | solution.py:299
  16.8 12.1 %collective-permute-start.6 = (f32[1,2,32,512]{3,2,1,0:T(8,128)S(1)}, f32[1,2,32,512]{3,2,1,0:T(8,128)S(1)}, u32[]{:S(2)}, u32[]{:S(2)}) collective-permute-start(f32[1,2,32,512]{3,2,1,0:T(8,128)S(1)} %collective-permute-done.1.refs_2_.refs_1_), channel_id=1, source_target_pairs={{0,2},{1,3},{2,4},{3,5},{4,6},{5,7},{6,8},{7,9},{8,10},{9,11},{10,... | collective-permute-start | bytes 393224 | tf_op jit(solution)/shard_map/ppermute | solution.py:299
  16.8 1.2 %copy-start.1 = (f32[512,512]{1,0:T(8,128)S(1)}, f32[512,512]{1,0:T(8,128)}, u32[]{:S(2)}) copy-start(f32[512,512]{1,0:T(8,128)} %inverse_ref.1) | copy-start | bytes 3145732
  18.0 0.9 %copy-start.2 = (f32[2,512,32]{1,2,0:T(8,128)S(1)}, f32[2,512,32]{1,2,0:T(8,128)}, u32[]{:S(2)}) copy-start(f32[2,512,32]{1,2,0:T(8,128)} %param.4) | copy-start | bytes 393220
  24.5 7.8 %collective-permute-start.5 = (f32[1,2,32,512]{3,2,1,0:T(8,128)S(1)}, f32[1,2,32,512]{3,2,1,0:T(8,128)S(1)}, u32[]{:S(2)}, u32[]{:S(2)}) collective-permute-start(f32[1,2,32,512]{3,2,1,0:T(8,128)S(1)} %meet.4.refs_2_.refs_0_), channel_id=1, source_target_pairs={{0,32},{1,129},{2,34},{3,131},{4,36},{5,133},{6,38},{7,135},{8,40}... | collective-permute-start | bytes 393224 | tf_op jit(solution)/shard_map/ppermute | solution.py:251
  25.6 6.8 %collective-permute-start.4 = (f32[1,2,32,512]{3,2,1,0:T(8,128)S(1)}, f32[1,2,32,512]{3,2,1,0:T(8,128)S(1)}, u32[]{:S(2)}, u32[]{:S(2)}) collective-permute-start(f32[1,2,32,512]{3,2,1,0:T(8,128)S(1)} %meet.4.refs_2_.refs_0_), channel_id=1, source_target_pairs={{0,48},{1,193},{2,50},{3,195},{4,52},{5,197},{6,54},{7,199},{8,56}... | collective-permute-start | bytes 393224 | tf_op jit(solution)/shard_map/ppermute | solution.py:251
  25.6 6.8 %collective-permute-start.3 = (f32[1,2,32,512]{3,2,1,0:T(8,128)S(1)}, f32[1,2,32,512]{3,2,1,0:T(8,128)S(1)}, u32[]{:S(2)}, u32[]{:S(2)}) collective-permute-start(f32[1,2,32,512]{3,2,1,0:T(8,128)S(1)} %meet.4.refs_2_.refs_0_), channel_id=1, source_target_pairs={{0,16},{1,65},{2,18},{3,67},{4,20},{5,69},{6,22},{7,71},{8,24},{9,... | collective-permute-start | bytes 393224 | tf_op jit(solution)/shard_map/ppermute | solution.py:251
  28.9 6.8 %collective-permute-start.11 = (f32[1,2,32,512]{3,2,1,0:T(8,128)S(1)}, f32[1,2,32,512]{3,2,1,0:T(8,128)S(1)}, u32[]{:S(2)}, u32[]{:S(2)}) collective-permute-start(f32[1,2,32,512]{3,2,1,0:T(8,128)S(1)} %get-tuple-element.11.refs_4_.refs_3_), channel_id=1, source_target_pairs={{0,2},{1,3},{2,4},{3,5},{4,6},{5,7},{6,8},{7,9},{8,10},{9,11},{10,... | collective-permute-start | bytes 393224 | tf_op jit(solution)/shard_map/ppermute | solution.py:299
  29.0 6.7 %collective-permute-start.12 = (f32[1,2,32,512]{3,2,1,0:T(8,128)S(1)}, f32[1,2,32,512]{3,2,1,0:T(8,128)S(1)}, u32[]{:S(2)}, u32[]{:S(2)}) collective-permute-start(f32[1,2,32,512]{3,2,1,0:T(8,128)S(1)} %get-tuple-element.12.refs_5_.refs_4_), channel_id=1, source_target_pairs={{0,14},{1,15},{2,0},{3,1},{4,2},{5,3},{6,4},{7,5},{8,6},{9,7},{10,... | collective-permute-start | bytes 393224 | tf_op jit(solution)/shard_map/ppermute | solution.py:299
  35.8 12.9 %collective-permute-start.14 = (f32[7,2,32,512]{3,2,1,0:T(8,128)S(1)}, f32[7,2,32,512]{3,2,1,0:T(8,128)S(1)}, u32[]{:S(2)}, u32[]{:S(2)}) collective-permute-start(f32[7,2,32,512]{3,2,1,0:T(8,128)S(1)} %stack.3.refs_0_), channel_id=1, source_target_pairs={{0,1},{1,0},{2,3},{3,2},{4,5},{5,4},{6,7},{7,6},{8,9},{9,8},{10,11... | collective-permute-start | bytes 2752520 | tf_op jit(solution)/shard_map/ppermute | solution.py:302
  35.9 16.1 %collective-permute-start.10 = (f32[4,2,32,512]{3,2,1,0:T(8,128)S(1)}, f32[4,2,32,512]{3,2,1,0:T(8,128)S(1)}, u32[]{:S(2)}, u32[]{:S(2)}) collective-permute-start(f32[4,2,32,512]{3,2,1,0:T(8,128)S(1)} %stack.2.refs_7_.first_ref), channel_id=1, source_target_pairs={{0,128},{1,33},{2,130},{3,35},{4,132},{5,37},{6,134},{7,39},{8,136... | collective-permute-start | bytes 1572872 | tf_op jit(solution)/shard_map/ppermute | solution.py:251
  37.8 14.1 %collective-permute-start.9 = (f32[4,2,32,512]{3,2,1,0:T(8,128)S(1)}, f32[4,2,32,512]{3,2,1,0:T(8,128)S(1)}, u32[]{:S(2)}, u32[]{:S(2)}) collective-permute-start(f32[4,2,32,512]{3,2,1,0:T(8,128)S(1)} %stack.2.refs_7_.first_ref), channel_id=1, source_target_pairs={{0,192},{1,49},{2,194},{3,51},{4,196},{5,53},{6,198},{7,55},{8,200... | collective-permute-start | bytes 1572872 | tf_op jit(solution)/shard_map/ppermute | solution.py:251
  37.8 14.5 %collective-permute-start.8 = (f32[4,2,32,512]{3,2,1,0:T(8,128)S(1)}, f32[4,2,32,512]{3,2,1,0:T(8,128)S(1)}, u32[]{:S(2)}, u32[]{:S(2)}) collective-permute-start(f32[4,2,32,512]{3,2,1,0:T(8,128)S(1)} %stack.2.refs_7_.first_ref), channel_id=1, source_target_pairs={{0,64},{1,17},{2,66},{3,19},{4,68},{5,21},{6,70},{7,23},{8,72},{9,... | collective-permute-start | bytes 1572872 | tf_op jit(solution)/shard_map/ppermute | solution.py:251
  39.8 7.4 %collective-permute-start.13 = (f32[1,2,32,512]{3,2,1,0:T(8,128)S(1)}, f32[1,2,32,512]{3,2,1,0:T(8,128)S(1)}, u32[]{:S(2)}, u32[]{:S(2)}) collective-permute-start(f32[1,2,32,512]{3,2,1,0:T(8,128)S(1)} %slice.4), channel_id=1, source_target_pairs={{0,2},{1,3},{2,4},{3,5},{4,6},{5,7},{6,8},{7,9},{8,10},{9,11},{10,... | collective-permute-start | bytes 393224 | tf_op jit(solution)/shard_map/ppermute | solution.py:299
  47.2 1.4 %collective-permute-start.15 = (f32[1,2,32,512]{3,2,1,0:T(8,128)S(1)}, f32[1,2,32,512]{3,2,1,0:T(8,128)S(1)}, u32[]{:S(2)}, u32[]{:S(2)}) collective-permute-start(f32[1,2,32,512]{3,2,1,0:T(8,128)S(1)} %collective-permute-done.13.refs_1_), channel_id=1, source_target_pairs={{0,1},{1,0},{2,3},{3,2},{4,5},{5,4},{6,7},{7,6},{8,9},{9,8},{10,11... | collective-permute-start | bytes 393224 | tf_op jit(solution)/shard_map/ppermute | solution.py:302

commit v5 on v4

--- a/solution.py
+++ b/solution.py
@@ -335,7 +335,7 @@
     planar = [in_plane(m, turned) for m in ((0, 1), (0, -1), (0, 2))]
     two, six = meet([two, six], [turned])
     three, five = by(1, two), by(-1, six)
-    (first,) = stacked([turned] + planar, others=[two, six], hint=16777216)
+    (first,) = stacked([turned] + planar, hint=16777216)
     (same,) = stacked([kept, one, seven, two, six, three, five], others=[first])
     four = by(1, same[5:6])
     other, other_four = swap(same), swap(four)

time: 58.4 us -> 58.4 us (level)
  no operation moved by 1% of the time
where the time goes in v5:
time: 58.4 us; the launch traced here: 57.7 us
  starting transfers between devices  22.5 us (39%)
  waiting for transfers between devices  22 us (38%)
  Pallas kernels  10.1 us (17%)
  local copies, waits for them, and re-layouts  2.14 us (4%)
  between operations  0.92 us (2%)
    ppermute x7, waiting for transfers between devices, by(): return lax.ppermute(block, 'pcol', along_z(step))  16.5 us
    ppermute x7, starting transfers between devices, by(): return lax.ppermute(block, 'pcol', along_z(step))  13 us
    ppermute x6, starting transfers between devices, in_plane(): return lax.ppermute(piece, ('prow', 'pcol'), pairs)  8.36 us
    pallas_call x1, Pallas kernels, local(): pl.pallas_call(right_kernel, out_shape=jax.ShapeDtypeStruct(view.shape, j...  5.25 us
    ppermute x1, waiting for transfers between devices, local(): turned = lax.ppermute(piece, ('prow', 'pcol'), turn)  5.08 us
    pallas_call x1, Pallas kernels, local(): pl.pallas_call(functools.partial(left_kernel, ((0, 1, 7, 2, 6, 3, 5), (4,...  3.27 us
    unnamed x6, local copies, waits for them, and re-layouts  2.13 us
  transfers between devices with their start and end apart: 16, of which 7 were waited for; matrix products, arithmetic and copies ran while one was open for 0% of the time, Pallas kernels for 8%

profile of v5, /device:TPU:6, one launch (start us, length us, event | category | flops | bytes accessed | tf_op | source)
XLA Modules:
  0.0 57.7 jit_solution(16901720579988602421)
XLA Ops:
  0.6 0.0 copy-start
  0.6 5.9 %collective-permute-start.2 = (f32[1,2,32,512]{3,2,1,0:T(8,128)}, f32[1,2,32,512]{3,2,1,0:T(8,128)S(1)}, u32[]{:S(2)}, u32[]{:S(2)}) collective-permute-start(f32[1,2,32,512]{3,2,1,0:T(8,128)} %bitcast.17), channel_id=1, source_target_pairs={{0,14},{1,15},{2,0},{3,1},{4,2},{5,3},{6,4},{7,5},{8,6},{9,7},{10,... | collective-permute-start | bytes 393224 | tf_op jit(solution)/shard_map/ppermute | solution.py:299
  6.6 0.0 collective-permute-start.1
  6.6 0.7 %collective-permute-start = (f32[1,2,32,512]{3,2,1,0:T(8,128)}, f32[1,2,32,512]{3,2,1,0:T(8,128)S(1)}, u32[]{:S(2)}, u32[]{:S(2)}) collective-permute-start(f32[1,2,32,512]{3,2,1,0:T(8,128)} %bitcast.19), channel_id=1, source_target_pairs={{0,112},{1,224},{2,96},{3,32},{4,176},{5,144},{6,80},{7,128},{8,19... | collective-permute-start | bytes 393224 | tf_op jit(solution)/shard_map/ppermute | solution.py:330
  7.3 2.4 %collective-permute-done.2.refs_3_.refs_2_ = f32[1,2,32,512]{3,2,1,0:T(8,128)S(1)} collective-permute-done((f32[1,2,32,512]{3,2,1,0:T(8,128)}, f32[1,2,32,512]{3,2,1,0:T(8,128)S(1)}, u32[]{:S(2)}, u32[]{:S(2)}) %collective-permute-start.2) | collective-permute-done | bytes 131104 | tf_op jit(solution)/shard_map/ppermute | solution.py:299
  9.6 3.6 %collective-permute-start.10 = (f32[1,2,32,512]{3,2,1,0:T(8,128)S(1)}, f32[1,2,32,512]{3,2,1,0:T(8,128)S(1)}, u32[]{:S(2)}, u32[]{:S(2)}) collective-permute-start(f32[1,2,32,512]{3,2,1,0:T(8,128)S(1)} %collective-permute-done.2.refs_3_.refs_2_), channel_id=1, source_target_pairs={{0,14},{1,15},{2,0},{3,1},{4,2},{5,3},{6,4},{7,5},{8,6},{9,7},{10,... | collective-permute-start | bytes 393224 | tf_op jit(solution)/shard_map/ppermute | solution.py:299
  13.2 3.6 %collective-permute-done.1.refs_2_.refs_1_ = f32[1,2,32,512]{3,2,1,0:T(8,128)S(1)} collective-permute-done((f32[1,2,32,512]{3,2,1,0:T(8,128)}, f32[1,2,32,512]{3,2,1,0:T(8,128)S(1)}, u32[]{:S(2)}, u32[]{:S(2)}) %collective-permute-start.1) | collective-permute-done | bytes 131104 | tf_op jit(solution)/shard_map/ppermute | solution.py:299
  16.8 0.0 collective-permute-start.9
  16.8 0.0 copy-start.1
  16.8 1.2 %copy-done.1 = f32[512,512]{1,0:T(8,128)S(1)} copy-done((f32[512,512]{1,0:T(8,128)S(1)}, f32[512,512]{1,0:T(8,128)}, u32[]{:S(2)}) %copy-start.1) | copy-done | bytes 1048600
  18.0 0.0 copy-start.2
  18.0 0.9 %copy-done.2 = f32[2,512,32]{1,2,0:T(8,128)S(1)} copy-done((f32[2,512,32]{1,2,0:T(8,128)S(1)}, f32[2,512,32]{1,2,0:T(8,128)}, u32[]{:S(2)}) %copy-start.2) | copy-done | bytes 131096
  18.9 0.4 prepare.1
  19.3 5.1 %collective-permute-done.refs_0_ = f32[1,2,32,512]{3,2,1,0:T(8,128)S(1)} collective-permute-done((f32[1,2,32,512]{3,2,1,0:T(8,128)}, f32[1,2,32,512]{3,2,1,0:T(8,128)S(1)}, u32[]{:S(2)}, u32[]{:S(2)}) %collective-permute-start) | collective-permute-done | bytes 131104 | tf_op jit(solution)/shard_map/ppermute | solution.py:330
  24.5 1.2 %collective-permute-start.5 = (f32[1,2,32,512]{3,2,1,0:T(8,128)S(1)}, f32[1,2,32,512]{3,2,1,0:T(8,128)S(1)}, u32[]{:S(2)}, u32[]{:S(2)}) collective-permute-start(f32[1,2,32,512]{3,2,1,0:T(8,128)S(1)} %meet.4.refs_0_.refs_2_), channel_id=1, source_target_pairs={{0,32},{1,129},{2,34},{3,131},{4,36},{5,133},{6,38},{7,135},{8,40}... | collective-permute-start | bytes 393224 | tf_op jit(solution)/shard_map/ppermute | solution.py:251
  25.6 0.0 collective-permute-start.4
  25.6 3.2 %collective-permute-start.3 = (f32[1,2,32,512]{3,2,1,0:T(8,128)S(1)}, f32[1,2,32,512]{3,2,1,0:T(8,128)S(1)}, u32[]{:S(2)}, u32[]{:S(2)}) collective-permute-start(f32[1,2,32,512]{3,2,1,0:T(8,128)S(1)} %meet.4.refs_0_.refs_2_), channel_id=1, source_target_pairs={{0,16},{1,65},{2,18},{3,67},{4,20},{5,69},{6,22},{7,71},{8,24},{9,... | collective-permute-start | bytes 393224 | tf_op jit(solution)/shard_map/ppermute | solution.py:251
  28.9 0.0 collective-permute-done.10.refs_1_
  28.9 0.0 collective-permute-done.9.refs_0_
  28.9 0.1 collective-permute-start.11
  29.0 3.3 %collective-permute-start.12 = (f32[1,2,32,512]{3,2,1,0:T(8,128)S(1)}, f32[1,2,32,512]{3,2,1,0:T(8,128)S(1)}, u32[]{:S(2)}, u32[]{:S(2)}) collective-permute-start(f32[1,2,32,512]{3,2,1,0:T(8,128)S(1)} %get-tuple-element.13.refs_4_), channel_id=1, source_target_pairs={{0,14},{1,15},{2,0},{3,1},{4,2},{5,3},{6,4},{7,5},{8,6},{9,7},{10,... | collective-permute-start | bytes 393224 | tf_op jit(solution)/shard_map/ppermute | solution.py:299
  32.3 0.0 collective-permute-done.5.refs_3_
  32.3 0.1 collective-permute-done.4.refs_2_
  32.4 0.0 collective-permute-done.3.refs_1_
  32.5 3.2 %collective-permute-done.11.refs_5_ = f32[1,2,32,512]{3,2,1,0:T(8,128)S(1)} collective-permute-done((f32[1,2,32,512]{3,2,1,0:T(8,128)S(1)}, f32[1,2,32,512]{3,2,1,0:T(8,128)S(1)}, u32[]{:S(2)}, u32[]{:S(2)}) %collective-permute-start.11) | collective-permute-done | bytes 131104 | tf_op jit(solution)/shard_map/ppermute | solution.py:299
  35.7 0.0 collective-permute-done.12.refs_6_
  35.7 0.1 stack.3.refs_0_
  35.8 0.1 collective-permute-start.14
  35.9 1.9 %collective-permute-start.8 = (f32[4,2,32,512]{3,2,1,0:T(8,128)S(1)}, f32[4,2,32,512]{3,2,1,0:T(8,128)S(1)}, u32[]{:S(2)}, u32[]{:S(2)}) collective-permute-start(f32[4,2,32,512]{3,2,1,0:T(8,128)S(1)} %stack.2.refs_7_.first_ref), channel_id=1, source_target_pairs={{0,128},{1,33},{2,130},{3,35},{4,132},{5,37},{6,134},{7,39},{8,136... | collective-permute-start | bytes 1572872 | tf_op jit(solution)/shard_map/ppermute | solution.py:251
  37.8 0.0 collective-permute-start.7
  37.8 2.0 %collective-permute-start.6 = (f32[4,2,32,512]{3,2,1,0:T(8,128)S(1)}, f32[4,2,32,512]{3,2,1,0:T(8,128)S(1)}, u32[]{:S(2)}, u32[]{:S(2)}) collective-permute-start(f32[4,2,32,512]{3,2,1,0:T(8,128)S(1)} %stack.2.refs_7_.first_ref), channel_id=1, source_target_pairs={{0,64},{1,17},{2,66},{3,19},{4,68},{5,21},{6,70},{7,23},{8,72},{9,... | collective-permute-start | bytes 1572872 | tf_op jit(solution)/shard_map/ppermute | solution.py:251
  39.8 0.1 collective-permute-start.13
  39.9 7.3 %collective-permute-done.13.refs_1_ = f32[1,2,32,512]{3,2,1,0:T(8,128)S(1)} collective-permute-done((f32[1,2,32,512]{3,2,1,0:T(8,128)S(1)}, f32[1,2,32,512]{3,2,1,0:T(8,128)S(1)}, u32[]{:S(2)}, u32[]{:S(2)}) %collective-permute-start.13) | collective-permute-done | bytes 131104 | tf_op jit(solution)/shard_map/ppermute | solution.py:299
  47.2 0.4 collective-permute-start.15
  47.6 0.0 copy-done
  47.6 1.0 %load.1.tiles_ref = f32[3,512,512]{2,1,0:T(8,128)S(1)} custom-call(f32[8192,128]{1,0:T(8,128)S(1)} %bitcast.16), custom_call_target="tpu_custom_call" | custom-call | bytes 8388608 | tf_op jit(solution)/shard_map/load/pallas_call | solution.py:314
  48.6 0.0 collective-permute-done.15.refs_3_
  48.6 0.0 collective-permute-done.14.refs_2_
  48.6 3.3 %left.1 = (bf16[2,512,512]{2,1,0:T(8,128)(2,1)S(1)}, bf16[2,512,512]{2,1,0:T(8,128)(2,1)S(1)}, f32[1,2,32,512]{3,2,1,0:T(8,128)}) custom-call(f32[7,2,32,512]{3,2,1,0:T(8,128)S(1)} %stack.3.refs_0_, f32[1,2,32,512]{3,2,1,0:T(8,128)S(1)} %collective-permute-done.13.refs_1_, f32[7,2,32,512]{3,2,1,0:T(8,128)S(1)} %collective-permute-done.14.refs_2_, ...), custom_call_target="tpu_custom_call" | custom-call | flops 2684354560 | bytes 6291456 | tf_op jit(solution)/shard_map/left/pallas_call | solution.py:343
  51.9 0.0 collective-permute-done.8.fourth_ref
  51.9 0.0 collective-permute-done.7.third_ref
  51.9 0.3 collective-permute-done.6.second_ref
  52.2 5.3 %right.1 = f32[8192,128]{1,0:T(8,128)} custom-call(f32[4,2,32,512]{3,2,1,0:T(8,128)S(1)} %stack.2.refs_7_.first_ref, f32[4,2,32,512]{3,2,1,0:T(8,128)S(1)} %collective-permute-done.6.second_ref, f32[4,2,32,512]{3,2,1,0:T(8,128)S(1)} %collective-permute-done.7.third_ref, f32[4,2,32,512]{3,2,1,0:T(8,128)S(1)} %collective-permute-done.8.fourth_ref, ...), custom_call_target="tpu_custom_call" | custom-call | flops 2415919104 | bytes 12582912 | tf_op jit(solution)/shard_map/right/pallas_call | solution.py:358
  (5 shorter events, 0.1 us)
Async XLA Ops:
  0.6 47.0 %copy-start = (f32[2,512,2,512]{3,2,1,0:T(2,128)S(1)}, f32[2,512,2,512]{3,2,1,0:T(2,128)}, u32[]{:S(2)}) copy-start(f32[2,512,2,512]{3,2,1,0:T(2,128)} %param.3) | copy-start | bytes 12582916
  0.6 9.0 %collective-permute-start.2 = (f32[1,2,32,512]{3,2,1,0:T(8,128)}, f32[1,2,32,512]{3,2,1,0:T(8,128)S(1)}, u32[]{:S(2)}, u32[]{:S(2)}) collective-permute-start(f32[1,2,32,512]{3,2,1,0:T(8,128)} %bitcast.17), channel_id=1, source_target_pairs={{0,14},{1,15},{2,0},{3,1},{4,2},{5,3},{6,4},{7,5},{8,6},{9,7},{10,... | collective-permute-start | bytes 393224 | tf_op jit(solution)/shard_map/ppermute | solution.py:299
  6.6 10.2 %collective-permute-start.1 = (f32[1,2,32,512]{3,2,1,0:T(8,128)}, f32[1,2,32,512]{3,2,1,0:T(8,128)S(1)}, u32[]{:S(2)}, u32[]{:S(2)}) collective-permute-start(f32[1,2,32,512]{3,2,1,0:T(8,128)} %bitcast.18), channel_id=1, source_target_pairs={{0,2},{1,3},{2,4},{3,5},{4,6},{5,7},{6,8},{7,9},{8,10},{9,11},{10,... | collective-permute-start | bytes 393224 | tf_op jit(solution)/shard_map/ppermute | solution.py:299
  6.6 17.8 %collective-permute-start = (f32[1,2,32,512]{3,2,1,0:T(8,128)}, f32[1,2,32,512]{3,2,1,0:T(8,128)S(1)}, u32[]{:S(2)}, u32[]{:S(2)}) collective-permute-start(f32[1,2,32,512]{3,2,1,0:T(8,128)} %bitcast.19), channel_id=1, source_target_pairs={{0,112},{1,224},{2,96},{3,32},{4,176},{5,144},{6,80},{7,128},{8,19... | collective-permute-start | bytes 393224 | tf_op jit(solution)/shard_map/ppermute | solution.py:330
  9.6 19.2 %collective-permute-start.10 = (f32[1,2,32,512]{3,2,1,0:T(8,128)S(1)}, f32[1,2,32,512]{3,2,1,0:T(8,128)S(1)}, u32[]{:S(2)}, u32[]{:S(2)}) collective-permute-start(f32[1,2,32,512]{3,2,1,0:T(8,128)S(1)} %collective-permute-done.2.refs_3_.refs_2_), channel_id=1, source_target_pairs={{0,14},{1,15},{2,0},{3,1},{4,2},{5,3},{6,4},{7,5},{8,6},{9,7},{10,... | collective-permute-start | bytes 393224 | tf_op jit(solution)/shard_map/ppermute | solution.py:299
  16.8 12.1 %collective-permute-start.9 = (f32[1,2,32,512]{3,2,1,0:T(8,128)S(1)}, f32[1,2,32,512]{3,2,1,0:T(8,128)S(1)}, u32[]{:S(2)}, u32[]{:S(2)}) collective-permute-start(f32[1,2,32,512]{3,2,1,0:T(8,128)S(1)} %collective-permute-done.1.refs_2_.refs_1_), channel_id=1, source_target_pairs={{0,2},{1,3},{2,4},{3,5},{4,6},{5,7},{6,8},{7,9},{8,10},{9,11},{10,... | collective-permute-start | bytes 393224 | tf_op jit(solution)/shard_map/ppermute | solution.py:299
  16.8 1.2 %copy-start.1 = (f32[512,512]{1,0:T(8,128)S(1)}, f32[512,512]{1,0:T(8,128)}, u32[]{:S(2)}) copy-start(f32[512,512]{1,0:T(8,128)} %inverse_ref.1) | copy-start | bytes 3145732
  18.0 0.9 %copy-start.2 = (f32[2,512,32]{1,2,0:T(8,128)S(1)}, f32[2,512,32]{1,2,0:T(8,128)}, u32[]{:S(2)}) copy-start(f32[2,512,32]{1,2,0:T(8,128)} %param.4) | copy-start | bytes 393220
  24.5 7.8 %collective-permute-start.5 = (f32[1,2,32,512]{3,2,1,0:T(8,128)S(1)}, f32[1,2,32,512]{3,2,1,0:T(8,128)S(1)}, u32[]{:S(2)}, u32[]{:S(2)}) collective-permute-start(f32[1,2,32,512]{3,2,1,0:T(8,128)S(1)} %meet.4.refs_0_.refs_2_), channel_id=1, source_target_pairs={{0,32},{1,129},{2,34},{3,131},{4,36},{5,133},{6,38},{7,135},{8,40}... | collective-permute-start | bytes 393224 | tf_op jit(solution)/shard_map/ppermute | solution.py:251
  25.6 6.8 %collective-permute-start.4 = (f32[1,2,32,512]{3,2,1,0:T(8,128)S(1)}, f32[1,2,32,512]{3,2,1,0:T(8,128)S(1)}, u32[]{:S(2)}, u32[]{:S(2)}) collective-permute-start(f32[1,2,32,512]{3,2,1,0:T(8,128)S(1)} %meet.4.refs_0_.refs_2_), channel_id=1, source_target_pairs={{0,48},{1,193},{2,50},{3,195},{4,52},{5,197},{6,54},{7,199},{8,56}... | collective-permute-start | bytes 393224 | tf_op jit(solution)/shard_map/ppermute | solution.py:251
  25.6 6.8 %collective-permute-start.3 = (f32[1,2,32,512]{3,2,1,0:T(8,128)S(1)}, f32[1,2,32,512]{3,2,1,0:T(8,128)S(1)}, u32[]{:S(2)}, u32[]{:S(2)}) collective-permute-start(f32[1,2,32,512]{3,2,1,0:T(8,128)S(1)} %meet.4.refs_0_.refs_2_), channel_id=1, source_target_pairs={{0,16},{1,65},{2,18},{3,67},{4,20},{5,69},{6,22},{7,71},{8,24},{9,... | collective-permute-start | bytes 393224 | tf_op jit(solution)/shard_map/ppermute | solution.py:251
  28.9 6.8 %collective-permute-start.11 = (f32[1,2,32,512]{3,2,1,0:T(8,128)S(1)}, f32[1,2,32,512]{3,2,1,0:T(8,128)S(1)}, u32[]{:S(2)}, u32[]{:S(2)}) collective-permute-start(f32[1,2,32,512]{3,2,1,0:T(8,128)S(1)} %get-tuple-element.12.refs_3_), channel_id=1, source_target_pairs={{0,2},{1,3},{2,4},{3,5},{4,6},{5,7},{6,8},{7,9},{8,10},{9,11},{10,... | collective-permute-start | bytes 393224 | tf_op jit(solution)/shard_map/ppermute | solution.py:299
  29.0 6.7 %collective-permute-start.12 = (f32[1,2,32,512]{3,2,1,0:T(8,128)S(1)}, f32[1,2,32,512]{3,2,1,0:T(8,128)S(1)}, u32[]{:S(2)}, u32[]{:S(2)}) collective-permute-start(f32[1,2,32,512]{3,2,1,0:T(8,128)S(1)} %get-tuple-element.13.refs_4_), channel_id=1, source_target_pairs={{0,14},{1,15},{2,0},{3,1},{4,2},{5,3},{6,4},{7,5},{8,6},{9,7},{10,... | collective-permute-start | bytes 393224 | tf_op jit(solution)/shard_map/ppermute | solution.py:299
  35.8 12.9 %collective-permute-start.14 = (f32[7,2,32,512]{3,2,1,0:T(8,128)S(1)}, f32[7,2,32,512]{3,2,1,0:T(8,128)S(1)}, u32[]{:S(2)}, u32[]{:S(2)}) collective-permute-start(f32[7,2,32,512]{3,2,1,0:T(8,128)S(1)} %stack.3.refs_0_), channel_id=1, source_target_pairs={{0,1},{1,0},{2,3},{3,2},{4,5},{5,4},{6,7},{7,6},{8,9},{9,8},{10,11... | collective-permute-start | bytes 2752520 | tf_op jit(solution)/shard_map/ppermute | solution.py:302
  35.9 16.1 %collective-permute-start.8 = (f32[4,2,32,512]{3,2,1,0:T(8,128)S(1)}, f32[4,2,32,512]{3,2,1,0:T(8,128)S(1)}, u32[]{:S(2)}, u32[]{:S(2)}) collective-permute-start(f32[4,2,32,512]{3,2,1,0:T(8,128)S(1)} %stack.2.refs_7_.first_ref), channel_id=1, source_target_pairs={{0,128},{1,33},{2,130},{3,35},{4,132},{5,37},{6,134},{7,39},{8,136... | collective-permute-start | bytes 1572872 | tf_op jit(solution)/shard_map/ppermute | solution.py:251
  37.8 14.1 %collective-permute-start.7 = (f32[4,2,32,512]{3,2,1,0:T(8,128)S(1)}, f32[4,2,32,512]{3,2,1,0:T(8,128)S(1)}, u32[]{:S(2)}, u32[]{:S(2)}) collective-permute-start(f32[4,2,32,512]{3,2,1,0:T(8,128)S(1)} %stack.2.refs_7_.first_ref), channel_id=1, source_target_pairs={{0,192},{1,49},{2,194},{3,51},{4,196},{5,53},{6,198},{7,55},{8,200... | collective-permute-start | bytes 1572872 | tf_op jit(solution)/shard_map/ppermute | solution.py:251
  37.8 14.5 %collective-permute-start.6 = (f32[4,2,32,512]{3,2,1,0:T(8,128)S(1)}, f32[4,2,32,512]{3,2,1,0:T(8,128)S(1)}, u32[]{:S(2)}, u32[]{:S(2)}) collective-permute-start(f32[4,2,32,512]{3,2,1,0:T(8,128)S(1)} %stack.2.refs_7_.first_ref), channel_id=1, source_target_pairs={{0,64},{1,17},{2,66},{3,19},{4,68},{5,21},{6,70},{7,23},{8,72},{9,... | collective-permute-start | bytes 1572872 | tf_op jit(solution)/shard_map/ppermute | solution.py:251
  39.8 7.4 %collective-permute-start.13 = (f32[1,2,32,512]{3,2,1,0:T(8,128)S(1)}, f32[1,2,32,512]{3,2,1,0:T(8,128)S(1)}, u32[]{:S(2)}, u32[]{:S(2)}) collective-permute-start(f32[1,2,32,512]{3,2,1,0:T(8,128)S(1)} %slice.4), channel_id=1, source_target_pairs={{0,2},{1,3},{2,4},{3,5},{4,6},{5,7},{6,8},{7,9},{8,10},{9,11},{10,... | collective-permute-start | bytes 393224 | tf_op jit(solution)/shard_map/ppermute | solution.py:299
  47.2 1.4 %collective-permute-start.15 = (f32[1,2,32,512]{3,2,1,0:T(8,128)S(1)}, f32[1,2,32,512]{3,2,1,0:T(8,128)S(1)}, u32[]{:S(2)}, u32[]{:S(2)}) collective-permute-start(f32[1,2,32,512]{3,2,1,0:T(8,128)S(1)} %collective-permute-done.13.refs_1_), channel_id=1, source_target_pairs={{0,1},{1,0},{2,3},{3,2},{4,5},{5,4},{6,7},{7,6},{8,9},{9,8},{10,11... | collective-permute-start | bytes 393224 | tf_op jit(solution)/shard_map/ppermute | solution.py:302
